TPU v7x, 32 devices: a whole 2x2x4 slice. The times are simulated.
32 devices in a mesh: groups: 1, pool: 32 (over z, y, x, core).
Axes of the slice: x: 2, y: 2, z: 4, core: 2. Of those that a mesh axis runs over, the one named last changes fastest.
Arguments:
- tokens: bfloat16 [2048, 7168], P(('groups', 'pool')), may hold values from -6 to 6
- slot_ids: int32 [2048, 2], P(('groups', 'pool')), may hold values from 0 to 3, all different within a row; in each aligned block of 64 rows (0 to 63, 64 to 127, ...) at most 48 rows name the same one
- gate_codes: int32 [2048, 2], P(('groups', 'pool')), may hold values from 1 to 1024
- gate_up: bfloat16 [28672, 2048], P('pool'), may hold values from -0.0625 to 0.0625
- down_proj: bfloat16 [1024, 28672], P(None, 'pool'), may hold values from -0.1875 to 0.1875
Outputs:
- mixed: bfloat16 [2048, 7168], P(('groups', 'pool'))
Inputs may be any that keep to these rules, and one draw needn't show every extreme that they name: `slot_ids`: each token names 2 different slots. Of the 64 tokens of one device, at most 48 name any one slot, and in every draw some slot is named by exactly 48 tokens of some device.
All inputs are finite; a program needn't handle non-finite values.
Results may differ from a plain program's by a relative error of at most 0.0058.
Values may be sent and summed in bfloat16 or wider, within the bound.
A program may use at most 128 MiB of HBM per device.

v0:
```python
import jax
import jax.numpy as jnp
from jax import lax
from jax.sharding import PartitionSpec as P

SPAN = 8


def from_partner(value, axis, bit):
    mask = 2**bit
    pairs = [(source, source ^ mask) for source in range(lax.axis_size(axis))]
    return lax.ppermute(value, axis, pairs)


def on_device(tokens, slot_ids, gate_codes, gate_up, down_proj):
    pool_size = lax.axis_size("pool")
    slots = pool_size // SPAN
    tok_rows = tokens.shape[0]
    topk = slot_ids.shape[1]
    piece = tokens.shape[1] // SPAN
    hidden_units = down_proj.shape[0]
    capacity = min(tok_rows, 3 * tok_rows * topk // (2 * slots))
    levels = SPAN.bit_length() - 1
    member = lax.axis_index("pool") % SPAN
    flat_slot = slot_ids.reshape(-1)
    slot_hot = (flat_slot[:, None] == jnp.arange(slots, dtype=jnp.int32)[None, :]).astype(jnp.int32)
    earlier = jnp.cumsum(slot_hot, axis=0) - slot_hot
    place = jnp.sum(earlier * slot_hot, axis=1)
    target = (flat_slot * capacity + place).reshape(tok_rows, topk)
    buffer_rows = jnp.arange(slots * capacity, dtype=jnp.int32)
    picker = jnp.any(target[None, :, :] == buffer_rows[:, None, None], axis=2).astype(jnp.bfloat16)
    picker = picker.reshape(slots, capacity, tok_rows)
    pieces = tokens.reshape(tok_rows, SPAN, piece)
    outgoing = jnp.einsum("sct,tjd->sjcd", picker, pieces, preferred_element_type=jnp.float32)
    outgoing = outgoing.astype(jnp.bfloat16).reshape(pool_size, capacity, piece)
    received = lax.all_to_all(outgoing, "pool", split_axis=0, concat_axis=0, tiled=True)
    count = received.shape[1]
    rows = received.reshape(pool_size * count, piece)
    summed = jnp.dot(rows, gate_up, preferred_element_type=jnp.float32)
    for bit in range(levels):
        upper_side = member >> bit & 1 == 1
        half = summed.shape[0] // 2
        lower_rows = summed[:half]
        upper_rows = summed[half:]
        leaving = jnp.where(upper_side, lower_rows, upper_rows)
        staying = jnp.where(upper_side, upper_rows, lower_rows)
        summed = staying + from_partner(leaving, "pool", bit)
    for bit in reversed(range(levels)):
        upper_side = member >> bit & 1 == 1
        partner = from_partner(summed, "pool", bit)
        summed = jnp.where(
            upper_side,
            jnp.concatenate([partner, summed], axis=0),
            jnp.concatenate([summed, partner], axis=0),
        )
    hidden = (jax.nn.silu(summed[:, :hidden_units]) * summed[:, hidden_units:]).astype(jnp.bfloat16)
    result = jnp.dot(hidden, down_proj, preferred_element_type=jnp.float32).astype(jnp.bfloat16)
    result = result.reshape(pool_size, count, piece)
    returned = lax.all_to_all(result, "pool", split_axis=0, concat_axis=0, tiled=True)
    flat_back = returned.reshape(pool_size * capacity, piece)
    column_part = jnp.arange(SPAN, dtype=jnp.int32)
    lookup = (slot_ids[:, :, None] * SPAN + column_part[None, None, :]) * capacity + place.reshape(
        tok_rows, topk
    )[:, :, None]
    fetched = jnp.take(flat_back, lookup.reshape(-1), axis=0).reshape(tok_rows, topk, SPAN * piece)
    weight = gate_codes.astype(jnp.float32) / 1024.0
    mixed = jnp.zeros((tok_rows, SPAN * piece), jnp.float32)
    for choice_index in range(topk):
        mixed = mixed + weight[:, choice_index, None] * fetched[:, choice_index].astype(jnp.float32)
    return mixed.astype(jnp.bfloat16)


def solution(mesh):
    placed = (
        P(("groups", "pool"), None),
        P(("groups", "pool"), None),
        P(("groups", "pool"), None),
        P("pool", None),
        P(None, "pool"),
    )
    return jax.shard_map(
        on_device,
        mesh=mesh,
        in_specs=placed,
        out_specs=P(("groups", "pool"), None),
        check_vma=False,
    )
```

profile of v0, /device:TPU:8, one launch (start us, length us, event | category | flops | bytes accessed | tf_op | source)
XLA Modules:
  0.0 435.0 jit_solution(13333132757761224401)
XLA Ops:
  0.0 0.9 copy.37
  0.9 0.1 eq.42
  1.0 0.1 fusion.6
  1.1 0.2 reduce_window_sum.11
  1.3 0.2 select_reduce_fusion
  1.5 0.1 add.99
  1.6 0.1 copy.38
  1.7 0.7 multiply_add_fusion.1
  2.4 0.1 fusion.5
  2.5 0.1 copy.41
  2.6 3.6 convolution_convert_fusion.1
  6.2 6.1 %all-to-all-start = ((bf16[32,48,896]{2,1,0:T(8,128)(2,1)}), bf16[32,48,896]{2,1,0:T(8,128)(2,1)}, u32[]{:S(2)}, u32[]{:S(2)}) async-start(bf16[32,48,896]{2,1,0:T(8,128)(2,1)} %bitcast.41), calls=%async_computation | async-start | bytes 5505024 | tf_op jit(solution)/shard_map/all_to_all | solution.py:36
  12.4 60.3 %all-to-all-done = bf16[32,48,896]{2,1,0:T(8,128)(2,1)} async-done(((bf16[32,48,896]{2,1,0:T(8,128)(2,1)}), bf16[32,48,896]{2,1,0:T(8,128)(2,1)}, u32[]{:S(2)}, u32[]{:S(2)}) %all-to-all-start) | async-done | bytes 2752544 | tf_op jit(solution)/shard_map/all_to_all | solution.py:36
  72.7 9.7 %fusion.8 = f32[1536,2048]{1,0:T(8,128)S(1)} fusion(bf16[1536,896]{1,0:T(8,128)(2,1)} %bitcast.7, bf16[896,2048]{1,0:T(8,128)(2,1)} %param.8), kind=kOutput, calls=%fused_computation.39 | convolution fusion | flops 5637144576 | bytes 19005440 | tf_op jit(solution)/shard_map/dot_general | solution.py:39
  82.4 4.4 %slice_select_fusion = f32[768,2048]{1,0:T(8,128)} fusion(f32[1536,2048]{1,0:T(8,128)S(1)} %fusion.8, pred[]{:T(512)S(6)} %eq.46), kind=kLoop, calls=%fused_computation.6 | loop fusion | flops 1572864 | bytes 18874368 | tf_op jit(solution)/shard_map/jit(_where)/select_n | solution.py:45
  86.8 2.0 copy-done.1
  88.8 0.7 collective-permute-start
  89.5 10.1 %collective-permute-done = f32[768,2048]{1,0:T(8,128)} collective-permute-done((f32[768,2048]{1,0:T(8,128)}, f32[768,2048]{1,0:T(8,128)}, u32[]{:S(2)}, u32[]{:S(2)}) %collective-permute-start) | collective-permute-done | bytes 6291488 | tf_op jit(solution)/shard_map/ppermute | solution.py:12
  99.6 11.8 %select_add_fusion = f32[768,2048]{1,0:T(8,128)} fusion(f32[768,2048]{1,0:T(8,128)} %collective-permute-done, f32[1536,2048]{1,0:T(8,128)} %copy-done.1, pred[]{:T(512)S(6)} %eq.46), kind=kLoop, calls=%fused_computation.5 | loop fusion | flops 3145728 | bytes 25165824 | tf_op jit(solution)/shard_map/add | solution.py:47
  111.4 5.2 %slice_select_fusion.1 = f32[384,2048]{1,0:T(8,128)} fusion(f32[768,2048]{1,0:T(8,128)} %select_add_fusion, pred[]{:T(512)S(6)} %eq.47), kind=kLoop, calls=%fused_computation.10 | loop fusion | flops 786432 | bytes 9437185 | tf_op jit(solution)/shard_map/jit(_where)/select_n | solution.py:45
  116.6 1.5 collective-permute-start.1
  118.1 69.2 %collective-permute-done.1 = f32[384,2048]{1,0:T(8,128)} collective-permute-done((f32[384,2048]{1,0:T(8,128)}, f32[384,2048]{1,0:T(8,128)}, u32[]{:S(2)}, u32[]{:S(2)}) %collective-permute-start.1) | collective-permute-done | bytes 3145760 | tf_op jit(solution)/shard_map/ppermute | solution.py:12
  187.3 4.7 %select_add_fusion.1 = f32[384,2048]{1,0:T(8,128)S(1)} fusion(f32[384,2048]{1,0:T(8,128)} %collective-permute-done.1, f32[768,2048]{1,0:T(8,128)} %select_add_fusion, pred[]{:T(512)S(6)} %eq.47), kind=kLoop, calls=%fused_computation.9 | loop fusion | flops 1572864 | bytes 12582913 | tf_op jit(solution)/shard_map/add | solution.py:47
  192.0 0.2 slice_select_fusion.2
  192.1 1.0 collective-permute-start.2
  193.1 35.0 %collective-permute-done.2 = f32[192,2048]{1,0:T(8,128)S(1)} collective-permute-done((f32[192,2048]{1,0:T(8,128)S(1)}, f32[192,2048]{1,0:T(8,128)S(1)}, u32[]{:S(2)}, u32[]{:S(2)}) %collective-permute-start.2) | collective-permute-done | bytes 1572896 | tf_op jit(solution)/shard_map/ppermute | solution.py:12
  228.1 0.3 select_add_fusion.2
  228.4 0.7 collective-permute-start.3
  229.1 34.3 %collective-permute-done.3 = f32[192,2048]{1,0:T(8,128)S(1)} collective-permute-done((f32[192,2048]{1,0:T(8,128)S(1)}, f32[192,2048]{1,0:T(8,128)S(1)}, u32[]{:S(2)}, u32[]{:S(2)}) %collective-permute-start.3) | collective-permute-done | bytes 1572896 | tf_op jit(solution)/shard_map/ppermute | solution.py:12
  263.4 0.4 maximum_select_fusion.2
  263.8 1.6 collective-permute-start.4
  265.4 66.2 %collective-permute-done.4 = f32[384,2048]{1,0:T(8,128)S(1)} collective-permute-done((f32[384,2048]{1,0:T(8,128)S(1)}, f32[384,2048]{1,0:T(8,128)S(1)}, u32[]{:S(2)}, u32[]{:S(2)}) %collective-permute-start.4) | collective-permute-done | bytes 3145760 | tf_op jit(solution)/shard_map/ppermute | solution.py:12
  331.6 1.9 maximum_select_fusion.1
  333.6 0.1 collective-permute-start.5
  333.6 10.1 %collective-permute-done.5 = f32[768,2048]{1,0:T(8,128)S(1)} collective-permute-done((f32[768,2048]{1,0:T(8,128)S(1)}, f32[768,2048]{1,0:T(8,128)S(1)}, u32[]{:S(2)}, u32[]{:S(2)}) %collective-permute-start.5) | collective-permute-done | bytes 6291488 | tf_op jit(solution)/shard_map/ppermute | solution.py:12
  343.8 4.4 %maximum_select_fusion = f32[1536,2048]{1,0:T(8,128)S(1)} fusion(f32[768,2048]{1,0:T(8,128)S(1)} %maximum_select_fusion.1, f32[768,2048]{1,0:T(8,128)S(1)} %collective-permute-done.5, pred[]{:T(512)S(6)} %eq.46), kind=kLoop, calls=%fused_computation.1 | loop fusion | flops 9437184 | bytes 25165824 | tf_op jit(solution)/shard_map/jit(_where)/select_n | solution.py:51
  348.2 4.8 %convolution_convert_fusion = bf16[1536,896]{1,0:T(8,128)(2,1)} fusion(bf16[1024,896]{1,0:T(8,128)(2,1)S(1)} %copy-done, f32[1536,2048]{1,0:T(8,128)S(1)} %maximum_select_fusion), kind=kOutput, calls=%fused_computation.7 | convolution fusion | flops 2829385728 | bytes 17170432 | tf_op jit(solution)/shard_map/dot_general | solution.py:57
  353.1 5.5 %all-to-all-start.1 = ((bf16[32,48,896]{2,1,0:T(8,128)(2,1)}), bf16[32,48,896]{2,1,0:T(8,128)(2,1)}, u32[]{:S(2)}, u32[]{:S(2)}) async-start(bf16[32,48,896]{2,1,0:T(8,128)(2,1)} %bitcast.42), calls=%async_computation.1 | async-start | bytes 5505024 | tf_op jit(solution)/shard_map/all_to_all | solution.py:59
  358.6 0.1 copy.43
  358.7 0.1 add.110
  358.8 0.1 copy.39
  359.0 0.3 broadcast_in_dim.16
  359.3 1.8 broadcast_in_dim.17
  361.1 57.8 %all-to-all-done.1 = bf16[32,48,896]{2,1,0:T(8,128)(2,1)} async-done(((bf16[32,48,896]{2,1,0:T(8,128)(2,1)}), bf16[32,48,896]{2,1,0:T(8,128)(2,1)}, u32[]{:S(2)}, u32[]{:S(2)}) %all-to-all-start.1) | async-done | bytes 2752544 | tf_op jit(solution)/shard_map/all_to_all | solution.py:59
  418.9 7.9 %gather_fusion = bf16[1024,896]{1,0:T(8,128)(2,1)} fusion(bf16[1536,896]{1,0:T(8,128)(2,1)} %bitcast.9, s32[1024]{0:T(1024)S(1)} %broadcast_clamp_fusion), kind=kCustom, calls=%fused_computation | custom fusion | bytes 3674112 | tf_op jit(solution)/shard_map/jit(_take)/gather | solution.py:65
  426.7 4.8 %gather.7 = bf16[64,2,7168]{2,1,0:T(2,128)(2,1)} reshape(bf16[1024,896]{1,0:T(8,128)(2,1)} %gather_fusion) | data formatting | bytes 3670016 | tf_op jit(solution)/shard_map/jit(_take)/gather | solution.py:65
  431.5 2.2 copy_select_fusion
  433.7 1.3 fusion.3
  (13 shorter events, 0.1 us)
Async XLA Ops:
  0.0 348.2 %copy-start = (bf16[1024,896]{1,0:T(8,128)(2,1)S(1)}, bf16[1024,896]{1,0:T(8,128)(2,1)}, u32[]{:S(2)}) copy-start(bf16[1024,896]{1,0:T(8,128)(2,1)} %param.9) | copy-start | bytes 5505028
  6.2 66.4 %all-to-all-start = ((bf16[32,48,896]{2,1,0:T(8,128)(2,1)}), bf16[32,48,896]{2,1,0:T(8,128)(2,1)}, u32[]{:S(2)}, u32[]{:S(2)}) async-start(bf16[32,48,896]{2,1,0:T(8,128)(2,1)} %bitcast.41), calls=%async_computation | async-start | bytes 5505024 | tf_op jit(solution)/shard_map/all_to_all | solution.py:36
  82.4 6.4 %copy-start.1 = (f32[1536,2048]{1,0:T(8,128)}, f32[1536,2048]{1,0:T(8,128)S(1)}, u32[]{:S(2)}) copy-start(f32[1536,2048]{1,0:T(8,128)S(1)} %fusion.8) | copy-start | bytes 37748740
  88.8 10.8 %collective-permute-start = (f32[768,2048]{1,0:T(8,128)}, f32[768,2048]{1,0:T(8,128)}, u32[]{:S(2)}, u32[]{:S(2)}) collective-permute-start(f32[768,2048]{1,0:T(8,128)} %slice_select_fusion), channel_id=1, source_target_pairs={{0,1},{1,0},{2,3},{3,2},{4,5},{5,4},{6,7},{7,6},{8,9},{9,8},{10,11... | collective-permute-start | bytes 18874376 | tf_op jit(solution)/shard_map/ppermute | solution.py:12
  116.6 70.7 %collective-permute-start.1 = (f32[384,2048]{1,0:T(8,128)}, f32[384,2048]{1,0:T(8,128)}, u32[]{:S(2)}, u32[]{:S(2)}) collective-permute-start(f32[384,2048]{1,0:T(8,128)} %slice_select_fusion.1), channel_id=1, source_target_pairs={{0,2},{1,3},{2,0},{3,1},{4,6},{5,7},{6,4},{7,5},{8,10},{9,11},{10,... | collective-permute-start | bytes 9437192 | tf_op jit(solution)/shard_map/ppermute | solution.py:12
  192.1 35.9 %collective-permute-start.2 = (f32[192,2048]{1,0:T(8,128)S(1)}, f32[192,2048]{1,0:T(8,128)S(1)}, u32[]{:S(2)}, u32[]{:S(2)}) collective-permute-start(f32[192,2048]{1,0:T(8,128)S(1)} %slice_select_fusion.2), channel_id=1, source_target_pairs={{0,4},{1,5},{2,6},{3,7},{4,0},{5,1},{6,2},{7,3},{8,12},{9,13},{10,... | collective-permute-start | bytes 4718600 | tf_op jit(solution)/shard_map/ppermute | solution.py:12
  228.4 35.0 %collective-permute-start.3 = (f32[192,2048]{1,0:T(8,128)S(1)}, f32[192,2048]{1,0:T(8,128)S(1)}, u32[]{:S(2)}, u32[]{:S(2)}) collective-permute-start(f32[192,2048]{1,0:T(8,128)S(1)} %select_add_fusion.2), channel_id=1, source_target_pairs={{0,4},{1,5},{2,6},{3,7},{4,0},{5,1},{6,2},{7,3},{8,12},{9,13},{10,... | collective-permute-start | bytes 4718600 | tf_op jit(solution)/shard_map/ppermute | solution.py:12
  263.8 67.8 %collective-permute-start.4 = (f32[384,2048]{1,0:T(8,128)S(1)}, f32[384,2048]{1,0:T(8,128)S(1)}, u32[]{:S(2)}, u32[]{:S(2)}) collective-permute-start(f32[384,2048]{1,0:T(8,128)S(1)} %maximum_select_fusion.2), channel_id=1, source_target_pairs={{0,2},{1,3},{2,0},{3,1},{4,6},{5,7},{6,4},{7,5},{8,10},{9,11},{10,... | collective-permute-start | bytes 9437192 | tf_op jit(solution)/shard_map/ppermute | solution.py:12
  333.6 10.2 %collective-permute-start.5 = (f32[768,2048]{1,0:T(8,128)S(1)}, f32[768,2048]{1,0:T(8,128)S(1)}, u32[]{:S(2)}, u32[]{:S(2)}) collective-permute-start(f32[768,2048]{1,0:T(8,128)S(1)} %maximum_select_fusion.1), channel_id=1, source_target_pairs={{0,1},{1,0},{2,3},{3,2},{4,5},{5,4},{6,7},{7,6},{8,9},{9,8},{10,11... | collective-permute-start | bytes 18874376 | tf_op jit(solution)/shard_map/ppermute | solution.py:12
  353.1 8.0 %copy-start.3 = (s32[64,2]{0,1:T(2,128)S(1)}, s32[64,2]{0,1:T(2,128)}, u32[]{:S(2)}) copy-start(s32[64,2]{0,1:T(2,128)} %param.7) | copy-start | bytes 1540
  353.1 65.8 %all-to-all-start.1 = ((bf16[32,48,896]{2,1,0:T(8,128)(2,1)}), bf16[32,48,896]{2,1,0:T(8,128)(2,1)}, u32[]{:S(2)}, u32[]{:S(2)}) async-start(bf16[32,48,896]{2,1,0:T(8,128)(2,1)} %bitcast.42), calls=%async_computation.1 | async-start | bytes 5505024 | tf_op jit(solution)/shard_map/all_to_all | solution.py:59
  426.7 4.8 %copy-start.2 = (pred[64,2,7168]{2,0,1:T(8,128)(4,1)S(1)}, pred[64,2,7168]{2,0,1:T(8,128)(4,1)}, u32[]{:S(2)}) copy-start(pred[64,2,7168]{2,0,1:T(8,128)(4,1)} %broadcast_in_dim.17) | copy-start | bytes 2752516
where the time goes:
time: 439 us; the launch traced here: 435 us
  waiting for transfers between devices  343 us (78%)
  other arithmetic  38.1 us (9%)
  local copies, waits for them, and re-layouts  18.5 us (4%)
  matrix products  18.2 us (4%)
  starting transfers between devices  17.1 us (4%)
    ppermute x6, waiting for transfers between devices, from_partner(): return lax.ppermute(value, axis, pairs)  225 us
    all_to_all x1, waiting for transfers between devices, on_device(): lax.all_to_all(outgoing, 'pool', split_axis=0, concat_axis=0, tiled=True)  60.3 us
    all_to_all x1, waiting for transfers between devices, on_device(): lax.all_to_all(result, 'pool', split_axis=0, concat_axis=0, tiled=True)  57.8 us
    add x3, other arithmetic, on_device(): summed = staying + from_partner(leaving, 'pool', bit)  16.8 us
    gather x2, local copies, waits for them, and re-layouts, on_device(): jnp.take(flat_back, lookup.reshape(-1), axis=0)  12.7 us
    select_n x3, other arithmetic, on_device(): leaving = jnp.where(upper_side, lower_rows, upper_rows)  9.76 us
    dot_general x1, matrix products, on_device(): summed = jnp.dot(rows, gate_up, preferred_element_type=jnp.float32)  9.74 us
  transfers between devices with their start and end apart: 8, of which 8 were waited for; matrix products, arithmetic and copies ran while one was open for 1% of the time, Pallas kernels for 0%

commit v1 on v0

v1 whole, which is shorter than its diff:
```python
import jax
import jax.numpy as jnp
from jax import lax
from jax.sharding import PartitionSpec as P

SPAN = 8
BF = jnp.bfloat16
F32 = jnp.float32


def swap(value, mask):
    pairs = [(source, source ^ mask) for source in range(lax.axis_size("pool"))]
    return lax.ppermute(value, "pool", pairs)


def kept(value, side, axis):
    return lax.dynamic_index_in_dim(value, side, axis, keepdims=False)


def joined(mine, other, side, axis):
    return jnp.where(side == 1, jnp.stack([other, mine], axis), jnp.stack([mine, other], axis))


def reduce_rows(partial, core, x, y):
    half = partial.shape[-1] // 2
    grid = partial.reshape(2, 2, 2, -1, 2 * half)
    now = kept(grid, core, 0) + swap(kept(grid, 1 - core, 0).astype(BF), 1)
    first, second = now[..., :half], now[..., half:]
    first_in = swap(kept(first, 1 - x, 0).astype(BF), 2)
    second_in = swap(kept(second, 1 - y, 1).astype(BF), 4)
    first = kept(first, x, 0) + first_in
    second = kept(second, y, 1) + second_in
    first_in = swap(kept(first, 1 - y, 0).astype(BF), 4)
    second_in = swap(kept(second, 1 - x, 0).astype(BF), 2)
    return kept(first, y, 0) + first_in, kept(second, x, 0) + second_in


def gather_rows(hidden, core, x, y):
    half = hidden.shape[-1] // 2
    first, second = hidden[:, :half], hidden[:, half:]
    first_in, second_in = swap(first, 4), swap(second, 2)
    first = joined(first, first_in, y, 0)
    second = joined(second, second_in, x, 0)
    first_in, second_in = swap(first, 2), swap(second, 4)
    first = joined(first, first_in, x, 0)
    second = joined(second, second_in, y, 1)
    both = jnp.concatenate([first, second], axis=-1)
    both = joined(both, swap(both, 1), core, 0)
    return both.reshape(-1, 2 * half)


def on_device(tokens, slot_ids, gate_codes, gate_up, down_proj):
    pool_size = lax.axis_size("pool")
    slots = pool_size // SPAN
    tok_rows, width = tokens.shape
    topk = slot_ids.shape[1]
    piece = width // SPAN
    hidden_units = down_proj.shape[0]
    capacity = min(tok_rows, 3 * tok_rows * topk // (2 * slots))
    index = lax.axis_index("pool")
    member, own_slot = index % SPAN, index // SPAN
    core, x, y = member & 1, member >> 1 & 1, member >> 2 & 1
    planes = [[s * SPAN + m for m in range(SPAN)] for s in range(slots)]

    routing = jnp.concatenate([slot_ids, gate_codes], axis=1)
    routing = lax.all_gather(routing, "pool", axis_index_groups=planes)
    plane_slots, plane_codes = routing[..., :topk], routing[..., topk:]
    pieces = tokens.reshape(tok_rows, SPAN, piece).transpose(1, 0, 2)
    plane_tokens = lax.all_to_all(pieces, "pool", split_axis=0, concat_axis=0, axis_index_groups=planes, tiled=True)

    def routes(slot):
        named = plane_slots == slot
        taken = jnp.any(named, axis=2)
        place = jnp.cumsum(taken.astype(jnp.int32), axis=1) - 1
        code = jnp.sum(jnp.where(named, plane_codes, 0), axis=2)
        hot = (place[:, :, None] == jnp.arange(capacity)) & taken[:, :, None]
        return hot, code

    blocks, mixers = [], []
    for step in range(slots):
        hot, code = routes(own_slot ^ step)
        high = jnp.where(hot, (code // 32)[:, :, None], 0).astype(F32) / 32.0
        low = jnp.where(hot, (code % 32)[:, :, None], 0).astype(F32) / 1024.0
        mixers.append((high.astype(BF), low.astype(BF)))
        block = jnp.einsum("jtc,jtd->jcd", hot.astype(BF), plane_tokens, preferred_element_type=F32)
        blocks.append(block.astype(BF).reshape(SPAN * capacity, piece))

    order = [0] + list(reversed(range(1, slots)))
    arrived = {step: swap(blocks[step], step * SPAN) if step else blocks[step] for step in order}
    mixed = jnp.zeros((SPAN, tok_rows, piece), F32)
    for step in order:
        partial = jnp.dot(arrived[step], gate_up, preferred_element_type=F32)
        gate, up = reduce_rows(partial, core, x, y)
        hidden = gather_rows((jax.nn.silu(gate) * up).astype(BF), core, x, y)
        result = jnp.dot(hidden, down_proj, preferred_element_type=F32).astype(BF)
        back = (swap(result, step * SPAN) if step else result).reshape(SPAN, capacity, piece)
        for part in mixers[step]:
            mixed = mixed + jnp.einsum("jtc,jcd->jtd", part, back, preferred_element_type=F32)
    out = lax.all_to_all(mixed.astype(BF), "pool", split_axis=0, concat_axis=0, axis_index_groups=planes, tiled=True)
    return out.transpose(1, 0, 2).reshape(tok_rows, width)


def solution(mesh):
    rows = P(("groups", "pool"), None)
    return jax.shard_map(
        on_device,
        mesh=mesh,
        in_specs=(rows, rows, rows, P("pool", None), P(None, "pool")),
        out_specs=rows,
        check_vma=False,
    )
```

time: 439 us -> 228 us (0.52)
  waiting for transfers between devices: 343 us -> 119 us
  other arithmetic: 38.1 us -> 3.97 us
  blocking collectives: 0 us -> 33.5 us
  starting transfers between devices: 17.1 us -> 49 us
  local copies, waits for them, and re-layouts: 18.5 us -> 4.96 us
    all_to_all x2 -> x1, waiting for transfers between devices: 118 us -> 0.01 us  [on_device(): lax.all_to_all(pieces, 'pool', split_axis=0, concat_axis=0, axis_index_gr...]
    ppermute x6 -> x46, waiting for transfers between devices: 225 us -> 119 us  [swap(): return lax.ppermute(value, 'pool', pairs)]
    ppermute x6 -> x46, starting transfers between devices: 5.52 us -> 45.3 us  [swap(): return lax.ppermute(value, 'pool', pairs)]
    select_n x8 -> x35, other arithmetic: 18.7 us -> 1.05 us  [the longest x31 1.01 us: joined(): jnp.where(side == 1, jnp.stack([other, mine], axis), jnp.stack([mine, oth...]
    all_gather x0 -> x1, blocking collectives: none -> 17.1 us  [on_device(): routing = lax.all_gather(routing, 'pool', axis_index_groups=planes)]
    all_to_all x0 -> x1, blocking collectives: none -> 16.5 us  [on_device(): lax.all_to_all(mixed.astype(BF), 'pool', split_axis=0, concat_axis=0, axi...]
    add x5 -> x12, other arithmetic: 17.5 us -> 1.17 us  [the longest x4 0.84 us: reduce_rows(): now = kept(grid, core, 0) + swap(kept(grid, 1 - core, 0).astype(BF), 1)]
    gather x2 -> x0, local copies, waits for them, and re-layouts: 12.7 us -> none  [on_device(): jnp.take(flat_back, lookup.reshape(-1), axis=0)]
  transfers between devices with their start and end apart: 8 -> 47, of which waited for: 8 -> 20; matrix products, arithmetic and copies ran while one was open for 1% -> 9% of each run, Pallas kernels for 0% -> 0%
where the time goes in v1:
time: 228 us
  waiting for transfers between devices  119 us (52%)
  starting transfers between devices  49 us (21%)
  blocking collectives  33.5 us (15%)
  matrix products  16.5 us (7%)
  local copies, waits for them, and re-layouts  4.96 us (2%)
  other arithmetic  3.97 us (2%)
    ppermute x46, waiting for transfers between devices, swap(): return lax.ppermute(value, 'pool', pairs)  119 us
    ppermute x46, starting transfers between devices, swap(): return lax.ppermute(value, 'pool', pairs)  45.3 us
    all_gather x1, blocking collectives, on_device(): routing = lax.all_gather(routing, 'pool', axis_index_groups=planes)  17.1 us
    all_to_all x1, blocking collectives, on_device(): lax.all_to_all(mixed.astype(BF), 'pool', split_axis=0, concat_axis=0, axi...  16.5 us
    dot_general x4, matrix products, on_device(): partial = jnp.dot(arrived[step], gate_up, preferred_element_type=F32)  7.14 us
  transfers between devices with their start and end apart: 47, of which 20 were waited for; matrix products, arithmetic and copies ran while one was open for 9% of the time, Pallas kernels for 0%

profile of v1, /device:TPU:8, one launch (start us, length us, event | category | flops | bytes accessed | tf_op | source)
XLA Modules:
  0.0 227.6 jit_solution(12374358524568729803)
XLA Ops:
  0.0 2.4 %copy.85 = bf16[8,8,8,896]{3,2,0,1:T(8,128)(2,1)} copy(bf16[8,8,8,896]{3,2,1,0:T(8,128)(2,1)} %bitcast.261) | data formatting | bytes 1835008 | tf_op jit(solution)/shard_map/reshape | solution.py:68
  2.4 3.7 %all-to-all-start = ((bf16[8,64,896]{2,1,0:T(8,128)(2,1)}), bf16[8,64,896]{2,1,0:T(8,128)(2,1)S(1)}, u32[]{:S(2)}, u32[]{:S(2)}) async-start(bf16[8,64,896]{2,1,0:T(8,128)(2,1)} %bitcast.245), calls=%async_computation | async-start | bytes 1835008 | tf_op jit(solution)/shard_map/all_to_all | solution.py:69
  6.1 17.1 %all-gather.1 = s32[8,64,4]{1,2,0:T(4,128)S(1)} all-gather(s32[1,64,4]{1,2,0:T(4,128)S(1)} %add_bitcast_fusion), channel_id=2, replica_groups={{0,1,2,3,4,5,6,7},{8,9,10,11,12,13,14,15},{16,17,18,19,20,21,22,23},{24..., dimensions={0}, use_global_device_ids=true | all-gather | bytes 9216 | tf_op jit(solution)/shard_map/all_gather | solution.py:66
  25.5 2.7 %collective-permute-start.22 = (bf16[384,896]{1,0:T(8,128)(2,1)S(1)}, bf16[384,896]{1,0:T(8,128)(2,1)S(1)}, u32[]{:S(2)}, u32[]{:S(2)}) collective-permute-start(bf16[384,896]{1,0:T(8,128)(2,1)S(1)} %bitcast.267), channel_id=1, source_target_pairs={{0,16},{1,17},{2,18},{3,19},{4,20},{5,21},{6,22},{7,23},{8,24},{9,... | collective-permute-start | bytes 2064392 | tf_op jit(solution)/shard_map/ppermute | solution.py:13
  29.3 1.8 fusion
  31.3 23.0 %collective-permute-done.34 = bf16[384,896]{1,0:T(8,128)(2,1)S(1)} collective-permute-done((bf16[384,896]{1,0:T(8,128)(2,1)S(1)}, bf16[384,896]{1,0:T(8,128)(2,1)S(1)}, u32[]{:S(2)}, u32[]{:S(2)}) %collective-permute-start.34) | collective-permute-done | bytes 688160 | tf_op jit(solution)/shard_map/ppermute | solution.py:13
  54.4 1.8 fusion.132
  56.4 17.1 %collective-permute-done.22 = bf16[384,896]{1,0:T(8,128)(2,1)S(1)} collective-permute-done((bf16[384,896]{1,0:T(8,128)(2,1)S(1)}, bf16[384,896]{1,0:T(8,128)(2,1)S(1)}, u32[]{:S(2)}, u32[]{:S(2)}) %collective-permute-start.22) | collective-permute-done | bytes 688160 | tf_op jit(solution)/shard_map/ppermute | solution.py:13
  73.5 1.8 fusion.131
  76.6 1.5 collective-permute-start.1
  78.1 3.4 %collective-permute-done.3 = bf16[2,48,1024]{2,1,0:T(8,128)(2,1)S(1)} collective-permute-done((bf16[2,48,1024]{2,1,0:T(8,128)(2,1)S(1)}, bf16[2,48,1024]{2,1,0:T(8,128)(2,1)S(1)}, u32[]{:S(2)}, u32[]{:S(2)}) %collective-permute-start.3) | collective-permute-done | bytes 196640 | tf_op jit(solution)/shard_map/ppermute | solution.py:13
  82.2 2.2 collective-permute-done.1
  84.4 1.5 collective-permute-start.2
  85.9 2.3 %collective-permute-done.10 = bf16[384,896]{1,0:T(8,128)(2,1)S(1)} collective-permute-done((bf16[384,896]{1,0:T(8,128)(2,1)S(1)}, bf16[384,896]{1,0:T(8,128)(2,1)S(1)}, u32[]{:S(2)}, u32[]{:S(2)}) %collective-permute-start.10) | collective-permute-done | bytes 688160 | tf_op jit(solution)/shard_map/ppermute | solution.py:13
  88.2 1.8 fusion.130
  91.0 1.5 collective-permute-start.5
  92.5 1.8 collective-permute-done.7
  95.2 1.9 collective-permute-start.6
  97.2 2.7 %collective-permute-done.6 = bf16[2,48,512]{2,1,0:T(8,128)(2,1)S(1)} collective-permute-done((bf16[2,48,512]{2,1,0:T(8,128)(2,1)S(1)}, bf16[2,48,512]{2,1,0:T(8,128)(2,1)S(1)}, u32[]{:S(2)}, u32[]{:S(2)}) %collective-permute-start.6) | collective-permute-done | bytes 98336 | tf_op jit(solution)/shard_map/ppermute | solution.py:13
  100.6 1.9 collective-permute-start.38
  103.2 1.9 collective-permute-start.26
  105.9 1.9 collective-permute-start.14
  107.9 1.0 convolution_convert_fusion.3
  110.3 1.9 collective-permute-start.39
  112.5 1.9 collective-permute-start.37
  114.9 1.9 collective-permute-done.14
  116.7 1.9 collective-permute-start.25
  119.1 1.8 collective-permute-done.39
  121.1 2.0 collective-permute-start.42
  123.3 2.0 collective-permute-start.30
  125.9 1.6 collective-permute-start.18
  127.8 1.7 collective-permute-start.16
  130.1 1.6 collective-permute-start.43
  132.3 1.6 collective-permute-start.31
  134.6 1.6 collective-permute-start.19
  136.3 2.4 %collective-permute-done.29 = bf16[2,48,512]{2,1,0:T(8,128)(2,1)S(1)} collective-permute-done((bf16[2,48,512]{2,1,0:T(8,128)(2,1)S(1)}, bf16[2,48,512]{2,1,0:T(8,128)(2,1)S(1)}, u32[]{:S(2)}, u32[]{:S(2)}) %collective-permute-start.29) | collective-permute-done | bytes 98336 | tf_op jit(solution)/shard_map/ppermute | solution.py:13
  138.7 0.7 collective-permute-start.17
  140.3 2.9 %collective-permute-done.17 = bf16[2,48,512]{2,1,0:T(8,128)(2,1)S(1)} collective-permute-done((bf16[2,48,512]{2,1,0:T(8,128)(2,1)S(1)}, bf16[2,48,512]{2,1,0:T(8,128)(2,1)S(1)}, u32[]{:S(2)}, u32[]{:S(2)}) %collective-permute-start.17) | collective-permute-done | bytes 98336 | tf_op jit(solution)/shard_map/ppermute | solution.py:13
  143.8 1.0 convolution_convert_fusion.1
  144.7 2.6 %collective-permute-start.33 = (bf16[384,896]{1,0:T(8,128)(2,1)S(1)}, bf16[384,896]{1,0:T(8,128)(2,1)S(1)}, u32[]{:S(2)}, u32[]{:S(2)}) collective-permute-start(bf16[384,896]{1,0:T(8,128)(2,1)S(1)} %convolution_convert_fusion.1), channel_id=1, source_target_pairs={{0,16},{1,17},{2,18},{3,19},{4,20},{5,21},{6,22},{7,23},{8,24},{9,... | collective-permute-start | bytes 2064392 | tf_op jit(solution)/shard_map/ppermute | solution.py:13
  147.5 1.0 convolution_convert_fusion.2
  149.1 1.0 convolution_convert_fusion
  150.1 1.5 collective-permute-start.45
  151.6 40.6 %collective-permute-done.33 = bf16[384,896]{1,0:T(8,128)(2,1)S(1)} collective-permute-done((bf16[384,896]{1,0:T(8,128)(2,1)S(1)}, bf16[384,896]{1,0:T(8,128)(2,1)S(1)}, u32[]{:S(2)}, u32[]{:S(2)}) %collective-permute-start.33) | collective-permute-done | bytes 688160 | tf_op jit(solution)/shard_map/ppermute | solution.py:13
  193.1 14.7 %collective-permute-done.21 = bf16[384,896]{1,0:T(8,128)(2,1)S(1)} collective-permute-done((bf16[384,896]{1,0:T(8,128)(2,1)S(1)}, bf16[384,896]{1,0:T(8,128)(2,1)S(1)}, u32[]{:S(2)}, u32[]{:S(2)}) %collective-permute-start.21) | collective-permute-done | bytes 688160 | tf_op jit(solution)/shard_map/ppermute | solution.py:13
  209.2 0.8 add_convert_fusion
  210.0 16.5 %all_to_all.10 = bf16[8,64,896]{2,1,0:T(8,128)(2,1)S(1)} all-to-all(bf16[8,64,896]{2,1,0:T(8,128)(2,1)S(1)} %add_convert_fusion), channel_id=1, replica_groups={{0,1,2,3,4,5,6,7},{8,9,10,11,12,13,14,15},{16,17,18,19,20,21,22,23},{24..., dimensions={0} | all-to-all | bytes 1835008 | tf_op jit(solution)/shard_map/all_to_all | solution.py:99
  226.5 1.1 copy.68
  (177 shorter events, 19.8 us)
Async XLA Ops:
  0.0 107.9 %copy-start = (bf16[1024,896]{1,0:T(8,128)(2,1)S(1)}, bf16[1024,896]{1,0:T(8,128)(2,1)}, u32[]{:S(2)}) copy-start(bf16[1024,896]{1,0:T(8,128)(2,1)} %param.9) | copy-start | bytes 5505028
  2.4 21.9 %all-to-all-start = ((bf16[8,64,896]{2,1,0:T(8,128)(2,1)}), bf16[8,64,896]{2,1,0:T(8,128)(2,1)S(1)}, u32[]{:S(2)}, u32[]{:S(2)}) async-start(bf16[8,64,896]{2,1,0:T(8,128)(2,1)} %bitcast.245), calls=%async_computation | async-start | bytes 1835008 | tf_op jit(solution)/shard_map/all_to_all | solution.py:69
  24.6 29.7 %collective-permute-start.34 = (bf16[384,896]{1,0:T(8,128)(2,1)S(1)}, bf16[384,896]{1,0:T(8,128)(2,1)S(1)}, u32[]{:S(2)}, u32[]{:S(2)}) collective-permute-start(bf16[384,896]{1,0:T(8,128)(2,1)S(1)} %bitcast.268), channel_id=1, source_target_pairs={{0,8},{1,9},{2,10},{3,11},{4,12},{5,13},{6,14},{7,15},{8,0},{9,1},... | collective-permute-start | bytes 2064392 | tf_op jit(solution)/shard_map/ppermute | solution.py:13
  25.5 48.0 %collective-permute-start.22 = (bf16[384,896]{1,0:T(8,128)(2,1)S(1)}, bf16[384,896]{1,0:T(8,128)(2,1)S(1)}, u32[]{:S(2)}, u32[]{:S(2)}) collective-permute-start(bf16[384,896]{1,0:T(8,128)(2,1)S(1)} %bitcast.267), channel_id=1, source_target_pairs={{0,16},{1,17},{2,18},{3,19},{4,20},{5,21},{6,22},{7,23},{8,24},{9,... | collective-permute-start | bytes 2064392 | tf_op jit(solution)/shard_map/ppermute | solution.py:13
  28.5 59.8 %collective-permute-start.10 = (bf16[384,896]{1,0:T(8,128)(2,1)S(1)}, bf16[384,896]{1,0:T(8,128)(2,1)S(1)}, u32[]{:S(2)}, u32[]{:S(2)}) collective-permute-start(bf16[384,896]{1,0:T(8,128)(2,1)S(1)} %bitcast.266), channel_id=1, source_target_pairs={{0,24},{1,25},{2,26},{3,27},{4,28},{5,29},{6,30},{7,31},{8,16},{9,... | collective-permute-start | bytes 2064392 | tf_op jit(solution)/shard_map/ppermute | solution.py:13
  31.2 44.0 %collective-permute-start = (bf16[2,2,48,2048]{3,2,1,0:T(8,128)(2,1)S(1)}, bf16[2,2,48,2048]{3,2,1,0:T(8,128)(2,1)S(1)}, u32[]{:S(2)}, u32[]{:S(2)}) collective-permute-start(bf16[2,2,48,2048]{3,2,1,0:T(8,128)(2,1)S(1)} %fusion.2), channel_id=1, source_target_pairs={{0,1},{1,0},{2,3},{3,2},{4,5},{5,4},{6,7},{7,6},{8,9},{9,8},{10,11... | collective-permute-start | bytes 2359304 | tf_op jit(solution)/shard_map/ppermute | solution.py:13
  56.3 43.9 %collective-permute-start.35 = (bf16[2,2,48,2048]{3,2,0,1:T(8,128)(2,1)S(1)}, bf16[2,2,48,2048]{3,2,0,1:T(8,128)(2,1)S(1)}, u32[]{:S(2)}, u32[]{:S(2)}) collective-permute-start(bf16[2,2,48,2048]{3,2,0,1:T(8,128)(2,1)S(1)} %fusion.5), channel_id=1, source_target_pairs={{0,1},{1,0},{2,3},{3,2},{4,5},{5,4},{6,7},{7,6},{8,9},{9,8},{10,11... | collective-permute-start | bytes 2359304 | tf_op jit(solution)/shard_map/ppermute | solution.py:13
  75.7 5.7 %collective-permute-start.3 = (bf16[2,48,1024]{2,1,0:T(8,128)(2,1)S(1)}, bf16[2,48,1024]{2,1,0:T(8,128)(2,1)S(1)}, u32[]{:S(2)}, u32[]{:S(2)}) collective-permute-start(bf16[2,48,1024]{2,1,0:T(8,128)(2,1)S(1)} %fusion.7), channel_id=1, source_target_pairs={{0,4},{1,5},{2,6},{3,7},{4,0},{5,1},{6,2},{7,3},{8,12},{9,13},{10,... | collective-permute-start | bytes 589832 | tf_op jit(solution)/shard_map/ppermute | solution.py:13
  76.5 26.3 %collective-permute-start.23 = (bf16[2,2,48,2048]{3,2,0,1:T(8,128)(2,1)S(1)}, bf16[2,2,48,2048]{3,2,0,1:T(8,128)(2,1)S(1)}, u32[]{:S(2)}, u32[]{:S(2)}) collective-permute-start(bf16[2,2,48,2048]{3,2,0,1:T(8,128)(2,1)S(1)} %fusion.4), channel_id=1, source_target_pairs={{0,1},{1,0},{2,3},{3,2},{4,5},{5,4},{6,7},{7,6},{8,9},{9,8},{10,11... | collective-permute-start | bytes 2359304 | tf_op jit(solution)/shard_map/ppermute | solution.py:13
  76.6 7.8 %collective-permute-start.1 = (bf16[2,48,1024]{2,1,0:T(8,128)(2,1)S(1)}, bf16[2,48,1024]{2,1,0:T(8,128)(2,1)S(1)}, u32[]{:S(2)}, u32[]{:S(2)}) collective-permute-start(bf16[2,48,1024]{2,1,0:T(8,128)(2,1)S(1)} %fusion.6), channel_id=1, source_target_pairs={{0,2},{1,3},{2,0},{3,1},{4,6},{5,7},{6,4},{7,5},{8,10},{9,11},{10,... | collective-permute-start | bytes 589832 | tf_op jit(solution)/shard_map/ppermute | solution.py:13
  81.5 8.5 %collective-permute-start.4 = (bf16[48,1024]{1,0:T(8,128)(2,1)S(1)}, bf16[48,1024]{1,0:T(8,128)(2,1)S(1)}, u32[]{:S(2)}, u32[]{:S(2)}) collective-permute-start(bf16[48,1024]{1,0:T(8,128)(2,1)S(1)} %fusion.32), channel_id=1, source_target_pairs={{0,2},{1,3},{2,0},{3,1},{4,6},{5,7},{6,4},{7,5},{8,10},{9,11},{10,... | collective-permute-start | bytes 294920 | tf_op jit(solution)/shard_map/ppermute | solution.py:13
  84.4 5.6 %collective-permute-start.2 = (bf16[48,1024]{1,0:T(8,128)(2,1)S(1)}, bf16[48,1024]{1,0:T(8,128)(2,1)S(1)}, u32[]{:S(2)}, u32[]{:S(2)}) collective-permute-start(bf16[48,1024]{1,0:T(8,128)(2,1)S(1)} %fusion.31), channel_id=1, source_target_pairs={{0,4},{1,5},{2,6},{3,7},{4,0},{5,1},{6,2},{7,3},{8,12},{9,13},{10,... | collective-permute-start | bytes 294920 | tf_op jit(solution)/shard_map/ppermute | solution.py:13
  90.2 4.2 %collective-permute-start.7 = (bf16[48,512]{1,0:T(8,128)(2,1)S(1)}, bf16[48,512]{1,0:T(8,128)(2,1)S(1)}, u32[]{:S(2)}, u32[]{:S(2)}) collective-permute-start(bf16[48,512]{1,0:T(8,128)(2,1)S(1)} %get-tuple-element.33), channel_id=1, source_target_pairs={{0,2},{1,3},{2,0},{3,1},{4,6},{5,7},{6,4},{7,5},{8,10},{9,11},{10,... | collective-permute-start | bytes 147464 | tf_op jit(solution)/shard_map/ppermute | solution.py:13
  91.0 14.2 %collective-permute-start.11 = (bf16[2,2,48,2048]{3,2,0,1:T(8,128)(2,1)S(1)}, bf16[2,2,48,2048]{3,2,0,1:T(8,128)(2,1)S(1)}, u32[]{:S(2)}, u32[]{:S(2)}) collective-permute-start(bf16[2,2,48,2048]{3,2,0,1:T(8,128)(2,1)S(1)} %fusion.3), channel_id=1, source_target_pairs={{0,1},{1,0},{2,3},{3,2},{4,5},{5,4},{6,7},{7,6},{8,9},{9,8},{10,11... | collective-permute-start | bytes 2359304 | tf_op jit(solution)/shard_map/ppermute | solution.py:13
  91.0 4.2 %collective-permute-start.5 = (bf16[48,512]{1,0:T(8,128)(2,1)S(1)}, bf16[48,512]{1,0:T(8,128)(2,1)S(1)}, u32[]{:S(2)}, u32[]{:S(2)}) collective-permute-start(bf16[48,512]{1,0:T(8,128)(2,1)S(1)} %get-tuple-element.34), channel_id=1, source_target_pairs={{0,4},{1,5},{2,6},{3,7},{4,0},{5,1},{6,2},{7,3},{8,12},{9,13},{10,... | collective-permute-start | bytes 147464 | tf_op jit(solution)/shard_map/ppermute | solution.py:13
  94.4 5.6 %collective-permute-start.8 = (bf16[2,48,512]{2,1,0:T(8,128)(2,1)S(1)}, bf16[2,48,512]{2,1,0:T(8,128)(2,1)S(1)}, u32[]{:S(2)}, u32[]{:S(2)}) collective-permute-start(bf16[2,48,512]{2,1,0:T(8,128)(2,1)S(1)} %maximum_select_fusion.14), channel_id=1, source_target_pairs={{0,4},{1,5},{2,6},{3,7},{4,0},{5,1},{6,2},{7,3},{8,12},{9,13},{10,... | collective-permute-start | bytes 294920 | tf_op jit(solution)/shard_map/ppermute | solution.py:13
  95.2 4.7 %collective-permute-start.6 = (bf16[2,48,512]{2,1,0:T(8,128)(2,1)S(1)}, bf16[2,48,512]{2,1,0:T(8,128)(2,1)S(1)}, u32[]{:S(2)}, u32[]{:S(2)}) collective-permute-start(bf16[2,48,512]{2,1,0:T(8,128)(2,1)S(1)} %maximum_select_fusion.12), channel_id=1, source_target_pairs={{0,2},{1,3},{2,0},{3,1},{4,6},{5,7},{6,4},{7,5},{8,10},{9,11},{10,... | collective-permute-start | bytes 294920 | tf_op jit(solution)/shard_map/ppermute | solution.py:13
  100.1 5.8 %collective-permute-start.9 = (bf16[2,2,48,1024]{3,2,1,0:T(8,128)(2,1)S(1)}, bf16[2,2,48,1024]{3,2,1,0:T(8,128)(2,1)S(1)}, u32[]{:S(2)}, u32[]{:S(2)}) collective-permute-start(bf16[2,2,48,1024]{3,2,1,0:T(8,128)(2,1)S(1)} %get-tuple-element.21), channel_id=1, source_target_pairs={{0,1},{1,0},{2,3},{3,2},{4,5},{5,4},{6,7},{7,6},{8,9},{9,8},{10,11... | collective-permute-start | bytes 1179656 | tf_op jit(solution)/shard_map/ppermute | solution.py:13
  100.6 9.4 %collective-permute-start.38 = (bf16[2,48,1024]{2,1,0:T(8,128)(2,1)S(1)}, bf16[2,48,1024]{2,1,0:T(8,128)(2,1)S(1)}, u32[]{:S(2)}, u32[]{:S(2)}) collective-permute-start(bf16[2,48,1024]{2,1,0:T(8,128)(2,1)S(1)} %fusion.13), channel_id=1, source_target_pairs={{0,4},{1,5},{2,6},{3,7},{4,0},{5,1},{6,2},{7,3},{8,12},{9,13},{10,... | collective-permute-start | bytes 589832 | tf_op jit(solution)/shard_map/ppermute | solution.py:13
  102.5 7.8 %collective-permute-start.36 = (bf16[2,48,1024]{2,1,0:T(8,128)(2,1)S(1)}, bf16[2,48,1024]{2,1,0:T(8,128)(2,1)S(1)}, u32[]{:S(2)}, u32[]{:S(2)}) collective-permute-start(bf16[2,48,1024]{2,1,0:T(8,128)(2,1)S(1)} %fusion.12), channel_id=1, source_target_pairs={{0,2},{1,3},{2,0},{3,1},{4,6},{5,7},{6,4},{7,5},{8,10},{9,11},{10,... | collective-permute-start | bytes 589832 | tf_op jit(solution)/shard_map/ppermute | solution.py:13
  103.2 9.3 %collective-permute-start.26 = (bf16[2,48,1024]{2,1,0:T(8,128)(2,1)S(1)}, bf16[2,48,1024]{2,1,0:T(8,128)(2,1)S(1)}, u32[]{:S(2)}, u32[]{:S(2)}) collective-permute-start(bf16[2,48,1024]{2,1,0:T(8,128)(2,1)S(1)} %fusion.11), channel_id=1, source_target_pairs={{0,4},{1,5},{2,6},{3,7},{4,0},{5,1},{6,2},{7,3},{8,12},{9,13},{10,... | collective-permute-start | bytes 589832 | tf_op jit(solution)/shard_map/ppermute | solution.py:13
  105.2 9.4 %collective-permute-start.24 = (bf16[2,48,1024]{2,1,0:T(8,128)(2,1)S(1)}, bf16[2,48,1024]{2,1,0:T(8,128)(2,1)S(1)}, u32[]{:S(2)}, u32[]{:S(2)}) collective-permute-start(bf16[2,48,1024]{2,1,0:T(8,128)(2,1)S(1)} %fusion.10), channel_id=1, source_target_pairs={{0,2},{1,3},{2,0},{3,1},{4,6},{5,7},{6,4},{7,5},{8,10},{9,11},{10,... | collective-permute-start | bytes 589832 | tf_op jit(solution)/shard_map/ppermute | solution.py:13
  105.9 10.9 %collective-permute-start.14 = (bf16[2,48,1024]{2,1,0:T(8,128)(2,1)S(1)}, bf16[2,48,1024]{2,1,0:T(8,128)(2,1)S(1)}, u32[]{:S(2)}, u32[]{:S(2)}) collective-permute-start(bf16[2,48,1024]{2,1,0:T(8,128)(2,1)S(1)} %fusion.9), channel_id=1, source_target_pairs={{0,4},{1,5},{2,6},{3,7},{4,0},{5,1},{6,2},{7,3},{8,12},{9,13},{10,... | collective-permute-start | bytes 589832 | tf_op jit(solution)/shard_map/ppermute | solution.py:13
  110.0 8.8 %collective-permute-start.12 = (bf16[2,48,1024]{2,1,0:T(8,128)(2,1)S(1)}, bf16[2,48,1024]{2,1,0:T(8,128)(2,1)S(1)}, u32[]{:S(2)}, u32[]{:S(2)}) collective-permute-start(bf16[2,48,1024]{2,1,0:T(8,128)(2,1)S(1)} %fusion.8), channel_id=1, source_target_pairs={{0,2},{1,3},{2,0},{3,1},{4,6},{5,7},{6,4},{7,5},{8,10},{9,11},{10,... | collective-permute-start | bytes 589832 | tf_op jit(solution)/shard_map/ppermute | solution.py:13
  110.3 10.5 %collective-permute-start.39 = (bf16[48,1024]{1,0:T(8,128)(2,1)S(1)}, bf16[48,1024]{1,0:T(8,128)(2,1)S(1)}, u32[]{:S(2)}, u32[]{:S(2)}) collective-permute-start(bf16[48,1024]{1,0:T(8,128)(2,1)S(1)} %fusion.44), channel_id=1, source_target_pairs={{0,2},{1,3},{2,0},{3,1},{4,6},{5,7},{6,4},{7,5},{8,10},{9,11},{10,... | collective-permute-start | bytes 294920 | tf_op jit(solution)/shard_map/ppermute | solution.py:13
  112.5 8.5 %collective-permute-start.37 = (bf16[48,1024]{1,0:T(8,128)(2,1)S(1)}, bf16[48,1024]{1,0:T(8,128)(2,1)S(1)}, u32[]{:S(2)}, u32[]{:S(2)}) collective-permute-start(bf16[48,1024]{1,0:T(8,128)(2,1)S(1)} %fusion.43), channel_id=1, source_target_pairs={{0,4},{1,5},{2,6},{3,7},{4,0},{5,1},{6,2},{7,3},{8,12},{9,13},{10,... | collective-permute-start | bytes 294920 | tf_op jit(solution)/shard_map/ppermute | solution.py:13
  114.5 8.5 %collective-permute-start.27 = (bf16[48,1024]{1,0:T(8,128)(2,1)S(1)}, bf16[48,1024]{1,0:T(8,128)(2,1)S(1)}, u32[]{:S(2)}, u32[]{:S(2)}) collective-permute-start(bf16[48,1024]{1,0:T(8,128)(2,1)S(1)} %fusion.40), channel_id=1, source_target_pairs={{0,2},{1,3},{2,0},{3,1},{4,6},{5,7},{6,4},{7,5},{8,10},{9,11},{10,... | collective-permute-start | bytes 294920 | tf_op jit(solution)/shard_map/ppermute | solution.py:13
  116.7 6.5 %collective-permute-start.25 = (bf16[48,1024]{1,0:T(8,128)(2,1)S(1)}, bf16[48,1024]{1,0:T(8,128)(2,1)S(1)}, u32[]{:S(2)}, u32[]{:S(2)}) collective-permute-start(bf16[48,1024]{1,0:T(8,128)(2,1)S(1)} %fusion.39), channel_id=1, source_target_pairs={{0,4},{1,5},{2,6},{3,7},{4,0},{5,1},{6,2},{7,3},{8,12},{9,13},{10,... | collective-permute-start | bytes 294920 | tf_op jit(solution)/shard_map/ppermute | solution.py:13
  118.8 6.6 %collective-permute-start.15 = (bf16[48,1024]{1,0:T(8,128)(2,1)S(1)}, bf16[48,1024]{1,0:T(8,128)(2,1)S(1)}, u32[]{:S(2)}, u32[]{:S(2)}) collective-permute-start(bf16[48,1024]{1,0:T(8,128)(2,1)S(1)} %fusion.36), channel_id=1, source_target_pairs={{0,2},{1,3},{2,0},{3,1},{4,6},{5,7},{6,4},{7,5},{8,10},{9,11},{10,... | collective-permute-start | bytes 294920 | tf_op jit(solution)/shard_map/ppermute | solution.py:13
  120.9 4.9 %collective-permute-start.13 = (bf16[48,1024]{1,0:T(8,128)(2,1)S(1)}, bf16[48,1024]{1,0:T(8,128)(2,1)S(1)}, u32[]{:S(2)}, u32[]{:S(2)}) collective-permute-start(bf16[48,1024]{1,0:T(8,128)(2,1)S(1)} %fusion.35), channel_id=1, source_target_pairs={{0,4},{1,5},{2,6},{3,7},{4,0},{5,1},{6,2},{7,3},{8,12},{9,13},{10,... | collective-permute-start | bytes 294920 | tf_op jit(solution)/shard_map/ppermute | solution.py:13
  121.1 9.0 %collective-permute-start.42 = (bf16[48,512]{1,0:T(8,128)(2,1)S(1)}, bf16[48,512]{1,0:T(8,128)(2,1)S(1)}, u32[]{:S(2)}, u32[]{:S(2)}) collective-permute-start(bf16[48,512]{1,0:T(8,128)(2,1)S(1)} %get-tuple-element.51), channel_id=1, source_target_pairs={{0,2},{1,3},{2,0},{3,1},{4,6},{5,7},{6,4},{7,5},{8,10},{9,11},{10,... | collective-permute-start | bytes 147464 | tf_op jit(solution)/shard_map/ppermute | solution.py:13
  123.1 8.7 %collective-permute-start.40 = (bf16[48,512]{1,0:T(8,128)(2,1)S(1)}, bf16[48,512]{1,0:T(8,128)(2,1)S(1)}, u32[]{:S(2)}, u32[]{:S(2)}) collective-permute-start(bf16[48,512]{1,0:T(8,128)(2,1)S(1)} %get-tuple-element.52), channel_id=1, source_target_pairs={{0,4},{1,5},{2,6},{3,7},{4,0},{5,1},{6,2},{7,3},{8,12},{9,13},{10,... | collective-permute-start | bytes 147464 | tf_op jit(solution)/shard_map/ppermute | solution.py:13
  123.3 4.4 %collective-permute-start.30 = (bf16[48,512]{1,0:T(8,128)(2,1)S(1)}, bf16[48,512]{1,0:T(8,128)(2,1)S(1)}, u32[]{:S(2)}, u32[]{:S(2)}) collective-permute-start(bf16[48,512]{1,0:T(8,128)(2,1)S(1)} %get-tuple-element.45), channel_id=1, source_target_pairs={{0,2},{1,3},{2,0},{3,1},{4,6},{5,7},{6,4},{7,5},{8,10},{9,11},{10,... | collective-permute-start | bytes 147464 | tf_op jit(solution)/shard_map/ppermute | solution.py:13
  125.3 8.6 %collective-permute-start.28 = (bf16[48,512]{1,0:T(8,128)(2,1)S(1)}, bf16[48,512]{1,0:T(8,128)(2,1)S(1)}, u32[]{:S(2)}, u32[]{:S(2)}) collective-permute-start(bf16[48,512]{1,0:T(8,128)(2,1)S(1)} %get-tuple-element.46), channel_id=1, source_target_pairs={{0,4},{1,5},{2,6},{3,7},{4,0},{5,1},{6,2},{7,3},{8,12},{9,13},{10,... | collective-permute-start | bytes 147464 | tf_op jit(solution)/shard_map/ppermute | solution.py:13
  125.9 4.2 %collective-permute-start.18 = (bf16[48,512]{1,0:T(8,128)(2,1)S(1)}, bf16[48,512]{1,0:T(8,128)(2,1)S(1)}, u32[]{:S(2)}, u32[]{:S(2)}) collective-permute-start(bf16[48,512]{1,0:T(8,128)(2,1)S(1)} %get-tuple-element.39), channel_id=1, source_target_pairs={{0,2},{1,3},{2,0},{3,1},{4,6},{5,7},{6,4},{7,5},{8,10},{9,11},{10,... | collective-permute-start | bytes 147464 | tf_op jit(solution)/shard_map/ppermute | solution.py:13
  127.8 6.8 %collective-permute-start.16 = (bf16[48,512]{1,0:T(8,128)(2,1)S(1)}, bf16[48,512]{1,0:T(8,128)(2,1)S(1)}, u32[]{:S(2)}, u32[]{:S(2)}) collective-permute-start(bf16[48,512]{1,0:T(8,128)(2,1)S(1)} %get-tuple-element.40), channel_id=1, source_target_pairs={{0,4},{1,5},{2,6},{3,7},{4,0},{5,1},{6,2},{7,3},{8,12},{9,13},{10,... | collective-permute-start | bytes 147464 | tf_op jit(solution)/shard_map/ppermute | solution.py:13
  130.1 9.5 %collective-permute-start.43 = (bf16[2,48,512]{2,1,0:T(8,128)(2,1)S(1)}, bf16[2,48,512]{2,1,0:T(8,128)(2,1)S(1)}, u32[]{:S(2)}, u32[]{:S(2)}) collective-permute-start(bf16[2,48,512]{2,1,0:T(8,128)(2,1)S(1)} %maximum_select_fusion.25), channel_id=1, source_target_pairs={{0,4},{1,5},{2,6},{3,7},{4,0},{5,1},{6,2},{7,3},{8,12},{9,13},{10,... | collective-permute-start | bytes 294920 | tf_op jit(solution)/shard_map/ppermute | solution.py:13
  131.8 7.9 %collective-permute-start.41 = (bf16[2,48,512]{2,1,0:T(8,128)(2,1)S(1)}, bf16[2,48,512]{2,1,0:T(8,128)(2,1)S(1)}, u32[]{:S(2)}, u32[]{:S(2)}) collective-permute-start(bf16[2,48,512]{2,1,0:T(8,128)(2,1)S(1)} %maximum_select_fusion.23), channel_id=1, source_target_pairs={{0,2},{1,3},{2,0},{3,1},{4,6},{5,7},{6,4},{7,5},{8,10},{9,11},{10,... | collective-permute-start | bytes 294920 | tf_op jit(solution)/shard_map/ppermute | solution.py:13
  132.3 7.0 %collective-permute-start.31 = (bf16[2,48,512]{2,1,0:T(8,128)(2,1)S(1)}, bf16[2,48,512]{2,1,0:T(8,128)(2,1)S(1)}, u32[]{:S(2)}, u32[]{:S(2)}) collective-permute-start(bf16[2,48,512]{2,1,0:T(8,128)(2,1)S(1)} %maximum_select_fusion.21), channel_id=1, source_target_pairs={{0,4},{1,5},{2,6},{3,7},{4,0},{5,1},{6,2},{7,3},{8,12},{9,13},{10,... | collective-permute-start | bytes 294920 | tf_op jit(solution)/shard_map/ppermute | solution.py:13
  134.0 4.7 %collective-permute-start.29 = (bf16[2,48,512]{2,1,0:T(8,128)(2,1)S(1)}, bf16[2,48,512]{2,1,0:T(8,128)(2,1)S(1)}, u32[]{:S(2)}, u32[]{:S(2)}) collective-permute-start(bf16[2,48,512]{2,1,0:T(8,128)(2,1)S(1)} %maximum_select_fusion.20), channel_id=1, source_target_pairs={{0,2},{1,3},{2,0},{3,1},{4,6},{5,7},{6,4},{7,5},{8,10},{9,11},{10,... | collective-permute-start | bytes 294920 | tf_op jit(solution)/shard_map/ppermute | solution.py:13
  134.6 8.7 %collective-permute-start.19 = (bf16[2,48,512]{2,1,0:T(8,128)(2,1)S(1)}, bf16[2,48,512]{2,1,0:T(8,128)(2,1)S(1)}, u32[]{:S(2)}, u32[]{:S(2)}) collective-permute-start(bf16[2,48,512]{2,1,0:T(8,128)(2,1)S(1)} %maximum_select_fusion.18), channel_id=1, source_target_pairs={{0,4},{1,5},{2,6},{3,7},{4,0},{5,1},{6,2},{7,3},{8,12},{9,13},{10,... | collective-permute-start | bytes 294920 | tf_op jit(solution)/shard_map/ppermute | solution.py:13
  138.7 4.6 %collective-permute-start.17 = (bf16[2,48,512]{2,1,0:T(8,128)(2,1)S(1)}, bf16[2,48,512]{2,1,0:T(8,128)(2,1)S(1)}, u32[]{:S(2)}, u32[]{:S(2)}) collective-permute-start(bf16[2,48,512]{2,1,0:T(8,128)(2,1)S(1)} %maximum_select_fusion.16), channel_id=1, source_target_pairs={{0,2},{1,3},{2,0},{3,1},{4,6},{5,7},{6,4},{7,5},{8,10},{9,11},{10,... | collective-permute-start | bytes 294920 | tf_op jit(solution)/shard_map/ppermute | solution.py:13
  139.5 4.0 %collective-permute-start.32 = (bf16[2,2,48,1024]{3,2,0,1:T(8,128)(2,1)S(1)}, bf16[2,2,48,1024]{3,2,0,1:T(8,128)(2,1)S(1)}, u32[]{:S(2)}, u32[]{:S(2)}) collective-permute-start(bf16[2,2,48,1024]{3,2,0,1:T(8,128)(2,1)S(1)} %get-tuple-element.25), channel_id=1, source_target_pairs={{0,1},{1,0},{2,3},{3,2},{4,5},{5,4},{6,7},{7,6},{8,9},{9,8},{10,11... | collective-permute-start | bytes 1179656 | tf_op jit(solution)/shard_map/ppermute | solution.py:13
  139.8 9.2 %collective-permute-start.44 = (bf16[2,2,48,1024]{3,2,1,0:T(8,128)(2,1)S(1)}, bf16[2,2,48,1024]{3,2,1,0:T(8,128)(2,1)S(1)}, u32[]{:S(2)}, u32[]{:S(2)}) collective-permute-start(bf16[2,2,48,1024]{3,2,1,0:T(8,128)(2,1)S(1)} %get-tuple-element.27), channel_id=1, source_target_pairs={{0,1},{1,0},{2,3},{3,2},{4,5},{5,4},{6,7},{7,6},{8,9},{9,8},{10,11... | collective-permute-start | bytes 1179656 | tf_op jit(solution)/shard_map/ppermute | solution.py:13
  143.5 3.9 %collective-permute-start.20 = (bf16[2,2,48,1024]{3,2,1,0:T(8,128)(2,1)S(1)}, bf16[2,2,48,1024]{3,2,1,0:T(8,128)(2,1)S(1)}, u32[]{:S(2)}, u32[]{:S(2)}) collective-permute-start(bf16[2,2,48,1024]{3,2,1,0:T(8,128)(2,1)S(1)} %get-tuple-element.23), channel_id=1, source_target_pairs={{0,1},{1,0},{2,3},{3,2},{4,5},{5,4},{6,7},{7,6},{8,9},{9,8},{10,11... | collective-permute-start | bytes 1179656 | tf_op jit(solution)/shard_map/ppermute | solution.py:13
  144.7 47.5 %collective-permute-start.33 = (bf16[384,896]{1,0:T(8,128)(2,1)S(1)}, bf16[384,896]{1,0:T(8,128)(2,1)S(1)}, u32[]{:S(2)}, u32[]{:S(2)}) collective-permute-start(bf16[384,896]{1,0:T(8,128)(2,1)S(1)} %convolution_convert_fusion.1), channel_id=1, source_target_pairs={{0,16},{1,17},{2,18},{3,19},{4,20},{5,21},{6,22},{7,23},{8,24},{9,... | collective-permute-start | bytes 2064392 | tf_op jit(solution)/shard_map/ppermute | solution.py:13
  148.4 59.4 %collective-permute-start.21 = (bf16[384,896]{1,0:T(8,128)(2,1)S(1)}, bf16[384,896]{1,0:T(8,128)(2,1)S(1)}, u32[]{:S(2)}, u32[]{:S(2)}) collective-permute-start(bf16[384,896]{1,0:T(8,128)(2,1)S(1)} %convolution_convert_fusion.2), channel_id=1, source_target_pairs={{0,24},{1,25},{2,26},{3,27},{4,28},{5,29},{6,30},{7,31},{8,16},{9,... | collective-permute-start | bytes 2064392 | tf_op jit(solution)/shard_map/ppermute | solution.py:13
  150.1 58.6 %collective-permute-start.45 = (bf16[384,896]{1,0:T(8,128)(2,1)S(1)}, bf16[384,896]{1,0:T(8,128)(2,1)S(1)}, u32[]{:S(2)}, u32[]{:S(2)}) collective-permute-start(bf16[384,896]{1,0:T(8,128)(2,1)S(1)} %convolution_convert_fusion), channel_id=1, source_target_pairs={{0,8},{1,9},{2,10},{3,11},{4,12},{5,13},{6,14},{7,15},{8,0},{9,1},... | collective-permute-start | bytes 2064392 | tf_op jit(solution)/shard_map/ppermute | solution.py:13
  (3 other events, 16.4 us)

commit v2 on v1

v2 whole, which is shorter than its diff:
```python
import functools
import jax
import jax.numpy as jnp
from jax import lax
from jax.experimental import pallas as pl
from jax.experimental.pallas import tpu as pltpu
from jax.sharding import PartitionSpec as P

SPAN = 8
BF = jnp.bfloat16
F32 = jnp.float32


def swap(value, mask):
    pairs = [(source, source ^ mask) for source in range(lax.axis_size("pool"))]
    return lax.ppermute(value, "pool", pairs)


def at(index, rows):
    return pl.ds(pl.multiple_of(index * rows, 16), rows)


def expert_kernel(cap, rows_ref, gate_up_ref, down_ref, out_ref, core_out, core_in, acc, wide_out, wide_in, thin_out, thin_in, hid, send_sems, recv_sems):
    me = lax.axis_index("pool")
    core, x, y = me % 2, me // 2 % 2, me // 4 % 2
    by_core, by_x, by_y = me + 1 - 2 * core, me + 2 - 4 * x, me + 4 - 8 * y
    units = acc.shape[1] // 2
    gate, up = pl.ds(0, units), pl.ds(units, units)
    fore, aft = pl.ds(0, units // 2), pl.ds(units // 2, units // 2)
    half = 4 * cap

    barrier = pltpu.get_barrier_semaphore()
    for partner in (by_core, by_x, by_y):
        pl.semaphore_signal(barrier, inc=1, device_id={"pool": partner}, device_id_type=pl.DeviceIdType.MESH)
    pl.semaphore_wait(barrier, 3)

    started = []

    def send(src, dst, partner):
        number = len(started)
        copy = pltpu.make_async_remote_copy(
            src_ref=src,
            dst_ref=dst,
            send_sem=send_sems.at[number],
            recv_sem=recv_sems.at[number],
            device_id={"pool": partner},
            device_id_type=pl.DeviceIdType.MESH,
        )
        copy.start()
        started.append(copy)
        return copy

    tile = units // 2
    crossing = []
    for side in (0, 1):

        @pl.loop(0, 2)
        def _(step, side=side):
            columns = pl.ds(pl.multiple_of(side * units + step * tile, tile), tile)
            core_out[:, columns] = jnp.dot(
                rows_ref[at(1 - core, half), :], gate_up_ref[:, columns], preferred_element_type=F32
            ).astype(BF)

        columns = (gate, up)[side]
        crossing.append(send(core_out.at[:, columns], core_in.at[:, columns], by_core))

    @pl.loop(0, 4)
    def _(step):
        columns = pl.ds(pl.multiple_of(step * tile, tile), tile)
        acc[:, columns] = jnp.dot(rows_ref[at(core, half), :], gate_up_ref[:, columns], preferred_element_type=F32)

    crossing[0].wait_recv()
    away = at(1 - x, 2 * cap)
    wide_out[0] = (acc[away, gate] + core_in[away, gate].astype(F32)).astype(BF)
    gate_one = send(wide_out.at[0], wide_in.at[0], by_x)
    crossing[1].wait_recv()
    for row in (0, 1):
        away = at(row * 2 + 1 - y, cap)
        wide_out[1, pl.ds(row * cap, cap), :] = (acc[away, up] + core_in[away, up].astype(F32)).astype(BF)
    up_one = send(wide_out.at[1], wide_in.at[1], by_y)

    gate_one.wait_recv()
    away = at(x * 2 + 1 - y, cap)
    thin_out[0] = (acc[away, gate] + core_in[away, gate].astype(F32) + wide_in[0, at(1 - y, cap), :].astype(F32)).astype(BF)
    gate_two = send(thin_out.at[0], thin_in.at[0], by_y)
    up_one.wait_recv()
    away = at((1 - x) * 2 + y, cap)
    thin_out[1] = (acc[away, up] + core_in[away, up].astype(F32) + wide_in[1, at(1 - x, cap), :].astype(F32)).astype(BF)
    up_two = send(thin_out.at[1], thin_in.at[1], by_x)

    home = at(x * 2 + y, cap)
    gate_two.wait_recv()
    gates = acc[home, gate] + core_in[home, gate].astype(F32) + wide_in[0, at(y, cap), :].astype(F32) + thin_in[0].astype(F32)
    gates = gates / (1.0 + jnp.exp(-gates))
    up_two.wait_recv()
    ups = acc[home, up] + core_in[home, up].astype(F32) + wide_in[1, at(x, cap), :].astype(F32) + thin_in[1].astype(F32)
    mine = at(core * 4 + x * 2 + y, cap)
    hid[mine, :] = (gates * ups).astype(BF)

    fore_y = send(hid.at[mine, fore], hid.at[mine, fore], by_y)
    aft_x = send(hid.at[mine, aft], hid.at[mine, aft], by_x)
    fore_x = send(hid.at[mine, fore], hid.at[mine, fore], by_x)
    aft_y = send(hid.at[mine, aft], hid.at[mine, aft], by_y)
    fore_y.wait_recv()
    theirs = at(core * 4 + x * 2 + 1 - y, cap)
    fore_on = send(hid.at[theirs, fore], hid.at[theirs, fore], by_x)
    aft_x.wait_recv()
    theirs = at(core * 4 + (1 - x) * 2 + y, cap)
    aft_on = send(hid.at[theirs, aft], hid.at[theirs, aft], by_y)
    for copy in (fore_x, aft_y, fore_on, aft_on):
        copy.wait_recv()
    mine = at(core, half)
    across = send(hid.at[mine, :], hid.at[mine, :], by_core)
    out_ref[mine, :] = jnp.dot(hid[mine, :], down_ref[...], preferred_element_type=F32).astype(BF)
    across.wait_recv()
    theirs = at(1 - core, half)
    out_ref[theirs, :] = jnp.dot(hid[theirs, :], down_ref[...], preferred_element_type=F32).astype(BF)
    for copy in started:
        copy.wait_send()


def expert(rows, gate_up, down):
    cap, units = rows.shape[0] // SPAN, down.shape[0]
    copies = 13
    flops = 2 * rows.shape[0] * rows.shape[1] * 3 * units
    return pl.pallas_call(
        functools.partial(expert_kernel, cap),
        out_shape=jax.ShapeDtypeStruct(rows.shape, BF),
        in_specs=[pl.BlockSpec(memory_space=pltpu.VMEM)] * 3,
        out_specs=pl.BlockSpec(memory_space=pltpu.VMEM),
        scratch_shapes=[
            pltpu.VMEM((4 * cap, 2 * units), BF),
            pltpu.VMEM((4 * cap, 2 * units), BF),
            pltpu.VMEM((4 * cap, 2 * units), F32),
            pltpu.VMEM((2, 2 * cap, units), BF),
            pltpu.VMEM((2, 2 * cap, units), BF),
            pltpu.VMEM((2, cap, units), BF),
            pltpu.VMEM((2, cap, units), BF),
            pltpu.VMEM((8 * cap, units), BF),
            pltpu.SemaphoreType.DMA((copies,)),
            pltpu.SemaphoreType.DMA((copies,)),
        ],
        compiler_params=pltpu.CompilerParams(collective_id=0, has_side_effects=True, vmem_limit_bytes=40 * 2**20),
        cost_estimate=pl.CostEstimate(flops=flops, bytes_accessed=40 * 2**20, transcendentals=0),
        name="expert",
    )(rows, gate_up, down)


def on_device(tokens, slot_ids, gate_codes, gate_up, down_proj):
    pool_size = lax.axis_size("pool")
    slots = pool_size // SPAN
    tok_rows, width = tokens.shape
    topk = slot_ids.shape[1]
    piece = width // SPAN
    capacity = min(tok_rows, 3 * tok_rows * topk // (2 * slots))
    capacity = -(-capacity // 16) * 16
    index = lax.axis_index("pool")
    own_slot = index // SPAN
    planes = [[s * SPAN + m for m in range(SPAN)] for s in range(slots)]

    routing = jnp.concatenate([slot_ids, gate_codes], axis=1)
    routing = lax.all_gather(routing, "pool", axis_index_groups=planes)
    plane_slots, plane_codes = routing[..., :topk], routing[..., topk:]
    pieces = tokens.reshape(tok_rows, SPAN, piece).transpose(1, 0, 2)
    plane_tokens = lax.all_to_all(pieces, "pool", split_axis=0, concat_axis=0, axis_index_groups=planes, tiled=True)

    def routes(slot):
        named = plane_slots == slot
        taken = jnp.any(named, axis=2)
        place = jnp.cumsum(taken.astype(jnp.int32), axis=1) - 1
        code = jnp.sum(jnp.where(named, plane_codes, 0), axis=2)
        hot = (place[:, :, None] == jnp.arange(capacity)) & taken[:, :, None]
        return hot, code

    blocks, mixers = [], []
    for step in range(slots):
        hot, code = routes(own_slot ^ step)
        high = jnp.where(hot, (code // 32)[:, :, None], 0).astype(F32) / 32.0
        low = jnp.where(hot, (code % 32)[:, :, None], 0).astype(F32) / 1024.0
        mixers.append((high.astype(BF), low.astype(BF)))
        block = jnp.einsum("jtc,jtd->jcd", hot.astype(BF), plane_tokens, preferred_element_type=F32)
        blocks.append(block.astype(BF).reshape(SPAN * capacity, piece))

    order = [0] + list(reversed(range(1, slots)))
    arrived = {step: swap(blocks[step], step * SPAN) if step else blocks[step] for step in order}
    mixed = jnp.zeros((SPAN, tok_rows, piece), F32)
    result = None
    for step in order:
        rows = arrived[step]
        if result is not None:
            rows, result = lax.optimization_barrier((rows, result))
        result = expert(rows, gate_up, down_proj)
        back = (swap(result, step * SPAN) if step else result).reshape(SPAN, capacity, piece)
        for part in mixers[step]:
            mixed = mixed + jnp.einsum("jtc,jcd->jtd", part, back, preferred_element_type=F32)
    out = lax.all_to_all(mixed.astype(BF), "pool", split_axis=0, concat_axis=0, axis_index_groups=planes, tiled=True)
    return out.transpose(1, 0, 2).reshape(tok_rows, width)


def solution(mesh):
    rows = P(("groups", "pool"), None)
    return jax.shard_map(
        on_device,
        mesh=mesh,
        in_specs=(rows, rows, rows, P("pool", None), P(None, "pool")),
        out_specs=rows,
        check_vma=False,
    )
```

time: 228 us -> 202 us (0.89)
  Pallas kernels: 0 us -> 88.7 us
  waiting for transfers between devices: 119 us -> 55.3 us
  starting transfers between devices: 49 us -> 12.3 us
  matrix products: 16.5 us -> 5.28 us
  other arithmetic: 3.97 us -> 1.08 us
    pallas_call x0 -> x4, Pallas kernels: none -> 88.7 us  [expert(): pl.pallas_call(functools.partial(expert_kernel, cap), out_shape=jax.Shape...]
    ppermute x46 -> x6, waiting for transfers between devices: 119 us -> 55.3 us  [swap(): return lax.ppermute(value, 'pool', pairs)]
    ppermute x46 -> x6, starting transfers between devices: 45.3 us -> 8.58 us  [swap(): return lax.ppermute(value, 'pool', pairs)]
    dot_general x8 -> x0, matrix products: 11 us -> none  [the longest x4 7.14 us: on_device(): partial = jnp.dot(arrived[step], gate_up, preferred_element_type=F32)]
  transfers between devices with their start and end apart: 47 -> 7, of which waited for: 20 -> 3; matrix products, arithmetic and copies ran while one was open for 9% -> 2% of each run, Pallas kernels for 0% -> 44%
where the time goes in v2:
time: 202 us; the launch traced here: 200 us
  Pallas kernels  88.7 us (44%)
  waiting for transfers between devices  55.3 us (27%)
  blocking collectives  33.5 us (17%)
  starting transfers between devices  12.3 us (6%)
  matrix products  5.28 us (3%)
  local copies, waits for them, and re-layouts  3.32 us (2%)
    pallas_call x4, Pallas kernels, expert(): pl.pallas_call(functools.partial(expert_kernel, cap), out_shape=jax.Shape...  88.7 us
    ppermute x6, waiting for transfers between devices, swap(): return lax.ppermute(value, 'pool', pairs)  55.3 us
    all_gather x1, blocking collectives, on_device(): routing = lax.all_gather(routing, 'pool', axis_index_groups=planes)  17.1 us
    all_to_all x1, blocking collectives, on_device(): lax.all_to_all(mixed.astype(BF), 'pool', split_axis=0, concat_axis=0, axi...  16.5 us
    ppermute x6, starting transfers between devices, swap(): return lax.ppermute(value, 'pool', pairs)  8.58 us
  transfers between devices with their start and end apart: 7, of which 3 were waited for; matrix products, arithmetic and copies ran while one was open for 2% of the time, Pallas kernels for 44%

profile of v2, /device:TPU:8, one launch (start us, length us, event | category | flops | bytes accessed | tf_op | source)
XLA Modules:
  0.0 199.7 jit_solution(11705382213009979067)
XLA Ops:
  0.0 0.0 copy-start.2
  0.0 0.0 copy-start.3
  0.0 2.3 %copy.13 = bf16[8,8,8,896]{3,2,0,1:T(8,128)(2,1)} copy(bf16[8,8,8,896]{3,2,1,0:T(8,128)(2,1)} %bitcast.42) | data formatting | bytes 1835008 | tf_op jit(solution)/shard_map/reshape | solution.py:164
  2.3 3.7 %all-to-all-start = ((bf16[8,64,896]{2,1,0:T(8,128)(2,1)}), bf16[8,64,896]{2,1,0:T(8,128)(2,1)S(1)}, u32[]{:S(2)}, u32[]{:S(2)}) async-start(bf16[8,64,896]{2,1,0:T(8,128)(2,1)} %bitcast.31), calls=%async_computation | async-start | bytes 1835008 | tf_op jit(solution)/shard_map/all_to_all | solution.py:165
  6.0 0.0 copy-done.2
  6.0 0.0 copy-done.3
  6.0 17.1 %all-gather.1 = s32[8,64,4]{1,2,0:T(4,128)S(1)} all-gather(s32[1,64,4]{1,2,0:T(4,128)S(1)} %add_bitcast_fusion), channel_id=2, replica_groups={{0,1,2,3,4,5,6,7},{8,9,10,11,12,13,14,15},{16,17,18,19,20,21,22,23},{24..., dimensions={0}, use_global_device_ids=true | all-gather | bytes 9216 | tf_op jit(solution)/shard_map/all_gather | solution.py:162
  23.1 0.1 fusion.88
  23.1 0.1 select_reduce_fusion.3
  23.2 0.2 reduce_window_sum.22
  23.4 0.2 reduce_window_sum.23
  23.7 0.2 reduce_window_sum.27
  23.9 0.2 reduce_window_sum.32
  24.2 0.0 all-to-all-done
  24.2 0.0 copy-start.1
  24.2 0.3 convolution_convert_fusion.2
  24.5 1.6 collective-permute-start
  26.2 0.0 copy-start
  26.2 0.3 convolution_convert_fusion.1
  26.5 1.3 collective-permute-start.2
  27.8 0.3 convolution_convert_fusion
  28.1 1.3 collective-permute-start.4
  29.5 0.3 convolution_convert_fusion.3
  29.8 0.0 copy-done.1
  29.8 0.0 copy-done
  29.8 21.5 %expert.4 = bf16[384,896]{1,0:T(8,128)(2,1)S(1)} custom-call(bf16[384,896]{1,0:T(8,128)(2,1)S(1)} %bitcast.34, bf16[896,2048]{1,0:T(8,128)(2,1)S(1)} %copy-done, bf16[1024,896]{1,0:T(8,128)(2,1)S(1)} %copy-done.1), custom_call_target="tpu_custom_call" | custom-call | flops 2113929216 | bytes 41943040 | tf_op jit(solution)/shard_map/expert/pallas_call | solution.py:126
  51.3 21.1 %collective-permute-done.rows_ref = bf16[384,896]{1,0:T(8,128)(2,1)S(1)} collective-permute-done((bf16[384,896]{1,0:T(8,128)(2,1)S(1)}, bf16[384,896]{1,0:T(8,128)(2,1)S(1)}, u32[]{:S(2)}, u32[]{:S(2)}) %collective-permute-start) | collective-permute-done | bytes 688160 | tf_op jit(solution)/shard_map/ppermute | solution.py:16
  72.3 21.4 %expert.5 = bf16[384,896]{1,0:T(8,128)(2,1)S(1)} custom-call(bf16[384,896]{1,0:T(8,128)(2,1)S(1)} %collective-permute-done.rows_ref, bf16[896,2048]{1,0:T(8,128)(2,1)S(1)} %copy-done, bf16[1024,896]{1,0:T(8,128)(2,1)S(1)} %copy-done.1), custom_call_target="tpu_custom_call" | custom-call | flops 2113929216 | bytes 41943040 | tf_op jit(solution)/shard_map/expert/pallas_call | solution.py:126
  93.8 0.0 collective-permute-done.2.rows_ref
  93.8 24.3 %expert.6 = bf16[384,896]{1,0:T(8,128)(2,1)S(1)} custom-call(bf16[384,896]{1,0:T(8,128)(2,1)S(1)} %collective-permute-done.2.rows_ref, bf16[896,2048]{1,0:T(8,128)(2,1)S(1)} %copy-done, bf16[1024,896]{1,0:T(8,128)(2,1)S(1)} %copy-done.1), custom_call_target="tpu_custom_call" | custom-call | flops 2113929216 | bytes 41943040 | tf_op jit(solution)/shard_map/expert/pallas_call | solution.py:126
  118.1 0.1 collective-permute-start.3
  118.1 0.5 fusion.9
  118.6 0.5 fusion.8
  119.1 1.6 collective-permute-start.1
  120.7 0.0 collective-permute-done.4.rows_ref
  120.7 21.5 %expert.7 = bf16[384,896]{1,0:T(8,128)(2,1)S(1)} custom-call(bf16[384,896]{1,0:T(8,128)(2,1)S(1)} %collective-permute-done.4.rows_ref, bf16[896,2048]{1,0:T(8,128)(2,1)S(1)} %copy-done, bf16[1024,896]{1,0:T(8,128)(2,1)S(1)} %copy-done.1), custom_call_target="tpu_custom_call" | custom-call | flops 2113929216 | bytes 41943040 | tf_op jit(solution)/shard_map/expert/pallas_call | solution.py:126
  142.2 2.6 %collective-permute-start.5 = (bf16[384,896]{1,0:T(8,128)(2,1)S(1)}, bf16[384,896]{1,0:T(8,128)(2,1)S(1)}, u32[]{:S(2)}, u32[]{:S(2)}) collective-permute-start(bf16[384,896]{1,0:T(8,128)(2,1)S(1)} %expert.7), channel_id=1, source_target_pairs={{0,8},{1,9},{2,10},{3,11},{4,12},{5,13},{6,14},{7,15},{8,0},{9,1},... | collective-permute-start | bytes 2064392 | tf_op jit(solution)/shard_map/ppermute | solution.py:16
  144.8 18.4 %collective-permute-done.3 = bf16[384,896]{1,0:T(8,128)(2,1)S(1)} collective-permute-done((bf16[384,896]{1,0:T(8,128)(2,1)S(1)}, bf16[384,896]{1,0:T(8,128)(2,1)S(1)}, u32[]{:S(2)}, u32[]{:S(2)}) %collective-permute-start.3) | collective-permute-done | bytes 688160 | tf_op jit(solution)/shard_map/ppermute | solution.py:16
  163.2 0.4 fusion.13
  163.7 0.5 fusion.12
  164.1 15.9 %collective-permute-done.1 = bf16[384,896]{1,0:T(8,128)(2,1)S(1)} collective-permute-done((bf16[384,896]{1,0:T(8,128)(2,1)S(1)}, bf16[384,896]{1,0:T(8,128)(2,1)S(1)}, u32[]{:S(2)}, u32[]{:S(2)}) %collective-permute-start.1) | collective-permute-done | bytes 688160 | tf_op jit(solution)/shard_map/ppermute | solution.py:16
  180.0 0.5 fusion.11
  180.4 0.5 fusion.10
  180.9 0.0 collective-permute-done.5
  180.9 0.5 fusion.14
  181.4 0.8 add_convert_fusion
  182.2 16.5 %all_to_all.10 = bf16[8,64,896]{2,1,0:T(8,128)(2,1)S(1)} all-to-all(bf16[8,64,896]{2,1,0:T(8,128)(2,1)S(1)} %add_convert_fusion), channel_id=1, replica_groups={{0,1,2,3,4,5,6,7},{8,9,10,11,12,13,14,15},{16,17,18,19,20,21,22,23},{24..., dimensions={0} | all-to-all | bytes 1835008 | tf_op jit(solution)/shard_map/all_to_all | solution.py:196
  198.7 1.1 copy.11
  (13 shorter events, 0.1 us)
Async XLA Ops:
  0.0 6.0 %copy-start.2 = (s32[64,2]{0,1:T(2,128)S(1)}, s32[64,2]{0,1:T(2,128)}, u32[]{:S(2)}) copy-start(s32[64,2]{0,1:T(2,128)} %param.7) | copy-start | bytes 1540
  0.0 6.0 %copy-start.3 = (s32[64,2]{0,1:T(2,128)S(1)}, s32[64,2]{0,1:T(2,128)}, u32[]{:S(2)}) copy-start(s32[64,2]{0,1:T(2,128)} %param.6) | copy-start | bytes 1540
  2.3 21.9 %all-to-all-start = ((bf16[8,64,896]{2,1,0:T(8,128)(2,1)}), bf16[8,64,896]{2,1,0:T(8,128)(2,1)S(1)}, u32[]{:S(2)}, u32[]{:S(2)}) async-start(bf16[8,64,896]{2,1,0:T(8,128)(2,1)} %bitcast.31), calls=%async_computation | async-start | bytes 1835008 | tf_op jit(solution)/shard_map/all_to_all | solution.py:165
  24.2 5.6 %copy-start.1 = (bf16[1024,896]{1,0:T(8,128)(2,1)S(1)}, bf16[1024,896]{1,0:T(8,128)(2,1)}, u32[]{:S(2)}) copy-start(bf16[1024,896]{1,0:T(8,128)(2,1)} %down_ref.7) | copy-start | bytes 5505028
  24.5 47.8 %collective-permute-start = (bf16[384,896]{1,0:T(8,128)(2,1)S(1)}, bf16[384,896]{1,0:T(8,128)(2,1)S(1)}, u32[]{:S(2)}, u32[]{:S(2)}) collective-permute-start(bf16[384,896]{1,0:T(8,128)(2,1)S(1)} %bitcast.45), channel_id=1, source_target_pairs={{0,24},{1,25},{2,26},{3,27},{4,28},{5,29},{6,30},{7,31},{8,16},{9,... | collective-permute-start | bytes 2064392 | tf_op jit(solution)/shard_map/ppermute | solution.py:16
  26.2 3.6 %copy-start = (bf16[896,2048]{1,0:T(8,128)(2,1)S(1)}, bf16[896,2048]{1,0:T(8,128)(2,1)}, u32[]{:S(2)}) copy-start(bf16[896,2048]{1,0:T(8,128)(2,1)} %gate_up_ref.7) | copy-start | bytes 11010052
  26.5 67.3 %collective-permute-start.2 = (bf16[384,896]{1,0:T(8,128)(2,1)S(1)}, bf16[384,896]{1,0:T(8,128)(2,1)S(1)}, u32[]{:S(2)}, u32[]{:S(2)}) collective-permute-start(bf16[384,896]{1,0:T(8,128)(2,1)S(1)} %bitcast.44), channel_id=1, source_target_pairs={{0,16},{1,17},{2,18},{3,19},{4,20},{5,21},{6,22},{7,23},{8,24},{9,... | collective-permute-start | bytes 2064392 | tf_op jit(solution)/shard_map/ppermute | solution.py:16
  28.1 92.5 %collective-permute-start.4 = (bf16[384,896]{1,0:T(8,128)(2,1)S(1)}, bf16[384,896]{1,0:T(8,128)(2,1)S(1)}, u32[]{:S(2)}, u32[]{:S(2)}) collective-permute-start(bf16[384,896]{1,0:T(8,128)(2,1)S(1)} %bitcast.43), channel_id=1, source_target_pairs={{0,8},{1,9},{2,10},{3,11},{4,12},{5,13},{6,14},{7,15},{8,0},{9,1},... | collective-permute-start | bytes 2064392 | tf_op jit(solution)/shard_map/ppermute | solution.py:16
  118.1 45.1 %collective-permute-start.3 = (bf16[384,896]{1,0:T(8,128)(2,1)S(1)}, bf16[384,896]{1,0:T(8,128)(2,1)S(1)}, u32[]{:S(2)}, u32[]{:S(2)}) collective-permute-start(bf16[384,896]{1,0:T(8,128)(2,1)S(1)} %expert.6), channel_id=1, source_target_pairs={{0,16},{1,17},{2,18},{3,19},{4,20},{5,21},{6,22},{7,23},{8,24},{9,... | collective-permute-start | bytes 2064392 | tf_op jit(solution)/shard_map/ppermute | solution.py:16
  119.1 60.9 %collective-permute-start.1 = (bf16[384,896]{1,0:T(8,128)(2,1)S(1)}, bf16[384,896]{1,0:T(8,128)(2,1)S(1)}, u32[]{:S(2)}, u32[]{:S(2)}) collective-permute-start(bf16[384,896]{1,0:T(8,128)(2,1)S(1)} %expert.5), channel_id=1, source_target_pairs={{0,24},{1,25},{2,26},{3,27},{4,28},{5,29},{6,30},{7,31},{8,16},{9,... | collective-permute-start | bytes 2064392 | tf_op jit(solution)/shard_map/ppermute | solution.py:16
  142.2 38.7 %collective-permute-start.5 = (bf16[384,896]{1,0:T(8,128)(2,1)S(1)}, bf16[384,896]{1,0:T(8,128)(2,1)S(1)}, u32[]{:S(2)}, u32[]{:S(2)}) collective-permute-start(bf16[384,896]{1,0:T(8,128)(2,1)S(1)} %expert.7), channel_id=1, source_target_pairs={{0,8},{1,9},{2,10},{3,11},{4,12},{5,13},{6,14},{7,15},{8,0},{9,1},... | collective-permute-start | bytes 2064392 | tf_op jit(solution)/shard_map/ppermute | solution.py:16

commit v3 on v1

v3 whole, which is shorter than its diff:
```python
import functools
import jax
import jax.numpy as jnp
from jax import lax
from jax.experimental import pallas as pl
from jax.experimental.pallas import tpu as pltpu
from jax.sharding import PartitionSpec as P

SPAN = 8
BF = jnp.bfloat16
F32 = jnp.float32


def at(index, rows):
    return pl.ds(pl.multiple_of(index * rows, 16), rows)


done = object()


def expert_kernel(cap, slots, rows_ref, gate_up_ref, down_ref, out_ref, came, results, core_outs, core_ins, accs, wide_outs, wide_ins, thin_outs, thin_ins, hids, send_sems, recv_sems):
    me = lax.axis_index("pool")
    core, x, y = me % 2, me // 2 % 2, me // 4 % 2
    by_core, by_x, by_y = me + 1 - 2 * core, me + 2 - 4 * x, me + 4 - 8 * y
    units = accs.shape[2] // 2
    gate, up = pl.ds(0, units), pl.ds(units, units)
    fore, aft = pl.ds(0, units // 2), pl.ds(units // 2, units // 2)
    half = 4 * cap

    def across_slots(step):
        partner = me
        for bit in range(slots.bit_length() - 1):
            if step >> bit & 1:
                mask = SPAN << bit
                partner = partner + mask - 2 * mask * (me // mask % 2)
        return partner

    barrier = pltpu.get_barrier_semaphore()
    partners = [by_core, by_x, by_y] + [across_slots(step) for step in range(1, slots)]
    for partner in partners:
        pl.semaphore_signal(barrier, inc=1, device_id={"pool": partner}, device_id_type=pl.DeviceIdType.MESH)
    pl.semaphore_wait(barrier, len(partners))

    started = []
    used = [0] * slots

    def send_for(step, src, dst, partner):
        number = used[step]
        used[step] += 1
        copy = pltpu.make_async_remote_copy(
            src_ref=src,
            dst_ref=dst,
            send_sem=send_sems.at[step, number],
            recv_sem=recv_sems.at[step, number],
            device_id={"pool": partner},
            device_id_type=pl.DeviceIdType.MESH,
        )
        copy.start()
        started.append(copy)
        return copy

    inbound, outbound = {}, []

    def dispatch(step):
        inbound[step] = send_for(step, rows_ref.at[step], came.at[step - 1], across_slots(step))

    def block(step):
        send = functools.partial(send_for, step)
        core_out, core_in, acc, wide_out, wide_in, thin_out, thin_in, hid = (
            ref.at[step] for ref in (core_outs, core_ins, accs, wide_outs, wide_ins, thin_outs, thin_ins, hids)
        )
        rows, result = rows_ref.at[0], out_ref.at[0]
        if step:
            rows, result = came.at[step - 1], results.at[step - 1]
            inbound[step].wait_recv()
        tile = units // 2
        crossing = []
        for side in (0, 1):

            @pl.loop(0, 2)
            def _(step, side=side):
                columns = pl.ds(pl.multiple_of(side * units + step * tile, tile), tile)
                core_out[:, columns] = jnp.dot(
                    rows[at(1 - core, half), :], gate_up_ref[:, columns], preferred_element_type=F32
                ).astype(BF)

            columns = (gate, up)[side]
            crossing.append(send(core_out.at[:, columns], core_in.at[:, columns], by_core))

        @pl.loop(0, 4)
        def _(step):
            columns = pl.ds(pl.multiple_of(step * tile, tile), tile)
            acc[:, columns] = jnp.dot(rows[at(core, half), :], gate_up_ref[:, columns], preferred_element_type=F32)

        yield
        crossing[0].wait_recv()
        away = at(1 - x, 2 * cap)
        wide_out[0] = (acc[away, gate] + core_in[away, gate].astype(F32)).astype(BF)
        gate_one = send(wide_out.at[0], wide_in.at[0], by_x)
        yield
        crossing[1].wait_recv()
        for row in (0, 1):
            away = at(row * 2 + 1 - y, cap)
            wide_out[1, pl.ds(row * cap, cap), :] = (acc[away, up] + core_in[away, up].astype(F32)).astype(BF)
        up_one = send(wide_out.at[1], wide_in.at[1], by_y)

        yield
        gate_one.wait_recv()
        away = at(x * 2 + 1 - y, cap)
        thin_out[0] = (acc[away, gate] + core_in[away, gate].astype(F32) + wide_in[0, at(1 - y, cap), :].astype(F32)).astype(BF)
        gate_two = send(thin_out.at[0], thin_in.at[0], by_y)
        yield
        up_one.wait_recv()
        away = at((1 - x) * 2 + y, cap)
        thin_out[1] = (acc[away, up] + core_in[away, up].astype(F32) + wide_in[1, at(1 - x, cap), :].astype(F32)).astype(BF)
        up_two = send(thin_out.at[1], thin_in.at[1], by_x)

        home = at(x * 2 + y, cap)
        yield
        gate_two.wait_recv()
        gates = acc[home, gate] + core_in[home, gate].astype(F32) + wide_in[0, at(y, cap), :].astype(F32) + thin_in[0].astype(F32)
        gates = gates / (1.0 + jnp.exp(-gates))
        yield
        up_two.wait_recv()
        ups = acc[home, up] + core_in[home, up].astype(F32) + wide_in[1, at(x, cap), :].astype(F32) + thin_in[1].astype(F32)
        mine = at(core * 4 + x * 2 + y, cap)
        hid[mine, :] = (gates * ups).astype(BF)

        fore_y = send(hid.at[mine, fore], hid.at[mine, fore], by_y)
        aft_x = send(hid.at[mine, aft], hid.at[mine, aft], by_x)
        fore_x = send(hid.at[mine, fore], hid.at[mine, fore], by_x)
        aft_y = send(hid.at[mine, aft], hid.at[mine, aft], by_y)
        yield
        fore_y.wait_recv()
        theirs = at(core * 4 + x * 2 + 1 - y, cap)
        fore_on = send(hid.at[theirs, fore], hid.at[theirs, fore], by_x)
        yield
        aft_x.wait_recv()
        theirs = at(core * 4 + (1 - x) * 2 + y, cap)
        aft_on = send(hid.at[theirs, aft], hid.at[theirs, aft], by_y)
        yield
        for copy in (fore_x, aft_y, fore_on, aft_on):
            copy.wait_recv()
        mine = at(core, half)
        across = send(hid.at[mine, :], hid.at[mine, :], by_core)
        result[mine, :] = jnp.dot(hid[mine, :], down_ref[...], preferred_element_type=F32).astype(BF)
        yield
        across.wait_recv()
        theirs = at(1 - core, half)
        result[theirs, :] = jnp.dot(hid[theirs, :], down_ref[...], preferred_element_type=F32).astype(BF)

        if step:
            outbound.append(send(result, out_ref.at[step], across_slots(step)))

    order = list(reversed(range(1, slots)))
    if slots > 1:
        dispatch(order[0])
    for _ in block(0):
        pass
    for step in order[1:]:
        dispatch(step)
    for group in [order[:1]] + [order[first : first + 2] for first in range(1, len(order), 2)]:
        running = [block(step) for step in group]
        while running:
            running = [work for work in running if next(work, done) is not done]
    for copy in outbound:
        copy.wait_recv()
    for copy in started:
        copy.wait_send()


def experts(rows, gate_up, down):
    slots, cap, units = rows.shape[0], rows.shape[1] // SPAN, down.shape[0]
    copies = 15
    flops = 2 * rows.shape[0] * rows.shape[1] * rows.shape[2] * 3 * units
    return pl.pallas_call(
        functools.partial(expert_kernel, cap, slots),
        out_shape=jax.ShapeDtypeStruct(rows.shape, BF),
        in_specs=[pl.BlockSpec(memory_space=pltpu.VMEM)] * 3,
        out_specs=pl.BlockSpec(memory_space=pltpu.VMEM),
        scratch_shapes=[
            pltpu.VMEM((max(1, slots - 1),) + rows.shape[1:], BF),
            pltpu.VMEM((max(1, slots - 1),) + rows.shape[1:], BF),
            pltpu.VMEM((slots, 4 * cap, 2 * units), BF),
            pltpu.VMEM((slots, 4 * cap, 2 * units), BF),
            pltpu.VMEM((slots, 4 * cap, 2 * units), F32),
            pltpu.VMEM((slots, 2, 2 * cap, units), BF),
            pltpu.VMEM((slots, 2, 2 * cap, units), BF),
            pltpu.VMEM((slots, 2, cap, units), BF),
            pltpu.VMEM((slots, 2, cap, units), BF),
            pltpu.VMEM((slots, 8 * cap, units), BF),
            pltpu.SemaphoreType.DMA((slots, copies)),
            pltpu.SemaphoreType.DMA((slots, copies)),
        ],
        compiler_params=pltpu.CompilerParams(collective_id=0, has_side_effects=True, vmem_limit_bytes=60 * 2**20),
        cost_estimate=pl.CostEstimate(flops=flops, bytes_accessed=40 * 2**20, transcendentals=0),
        name="experts",
    )(rows, gate_up, down)


def on_device(tokens, slot_ids, gate_codes, gate_up, down_proj):
    pool_size = lax.axis_size("pool")
    slots = pool_size // SPAN
    tok_rows, width = tokens.shape
    topk = slot_ids.shape[1]
    piece = width // SPAN
    capacity = min(tok_rows, 3 * tok_rows * topk // (2 * slots))
    capacity = -(-capacity // 16) * 16
    index = lax.axis_index("pool")
    own_slot = index // SPAN
    planes = [[s * SPAN + m for m in range(SPAN)] for s in range(slots)]

    routing = jnp.concatenate([slot_ids, gate_codes], axis=1)
    routing = lax.all_gather(routing, "pool", axis_index_groups=planes)
    plane_slots, plane_codes = routing[..., :topk], routing[..., topk:]
    pieces = tokens.reshape(tok_rows, SPAN, piece).transpose(1, 0, 2)
    plane_tokens = lax.all_to_all(pieces, "pool", split_axis=0, concat_axis=0, axis_index_groups=planes, tiled=True)

    def routes(slot):
        named = plane_slots == slot
        taken = jnp.any(named, axis=2)
        place = jnp.cumsum(taken.astype(jnp.int32), axis=1) - 1
        code = jnp.sum(jnp.where(named, plane_codes, 0), axis=2)
        hot = (place[:, :, None] == jnp.arange(capacity)) & taken[:, :, None]
        return hot, code

    blocks, mixers = [], []
    for step in range(slots):
        hot, code = routes(own_slot ^ step)
        high = jnp.where(hot, (code // 32)[:, :, None], 0).astype(F32) / 32.0
        low = jnp.where(hot, (code % 32)[:, :, None], 0).astype(F32) / 1024.0
        mixers.append((high.astype(BF), low.astype(BF)))
        block = jnp.einsum("jtc,jtd->jcd", hot.astype(BF), plane_tokens, preferred_element_type=F32)
        blocks.append(block.astype(BF).reshape(SPAN * capacity, piece))

    returned = experts(jnp.stack(blocks), gate_up, down_proj)
    mixed = jnp.zeros((SPAN, tok_rows, piece), F32)
    for step in range(slots):
        back = returned[step].reshape(SPAN, capacity, piece)
        for part in mixers[step]:
            mixed = mixed + jnp.einsum("jtc,jcd->jtd", part, back, preferred_element_type=F32)
    out = lax.all_to_all(mixed.astype(BF), "pool", split_axis=0, concat_axis=0, axis_index_groups=planes, tiled=True)
    return out.transpose(1, 0, 2).reshape(tok_rows, width)


def solution(mesh):
    rows = P(("groups", "pool"), None)
    return jax.shard_map(
        on_device,
        mesh=mesh,
        in_specs=(rows, rows, rows, P("pool", None), P(None, "pool")),
        out_specs=rows,
        check_vma=False,
    )
```

time: 228 us -> 199 us (0.87)
  Pallas kernels: 0 us -> 146 us
  waiting for transfers between devices: 119 us -> 0.01 us
  starting transfers between devices: 49 us -> 3.72 us
  matrix products: 16.5 us -> 5.29 us
    pallas_call x0 -> x1, Pallas kernels: none -> 146 us  [experts(): pl.pallas_call(functools.partial(expert_kernel, cap, slots), out_shape=ja...]
    ppermute x46 -> x0, waiting for transfers between devices: 119 us -> none  [swap(): return lax.ppermute(value, 'pool', pairs)]
    ppermute x46 -> x0, starting transfers between devices: 45.3 us -> none  [swap(): return lax.ppermute(value, 'pool', pairs)]
    dot_general x8 -> x0, matrix products: 11 us -> none  [the longest x4 7.14 us: on_device(): partial = jnp.dot(arrived[step], gate_up, preferred_element_type=F32)]
  transfers between devices with their start and end apart: 47 -> 1, of which waited for: 20 -> 0; matrix products, arithmetic and copies ran while one was open for 9% -> 1% of each run, Pallas kernels for 0% -> 0%
where the time goes in v3:
time: 199 us; the launch traced here: 198 us
  Pallas kernels  146 us (73%)
  blocking collectives  34.7 us (17%)
  matrix products  5.29 us (3%)
  local copies, waits for them, and re-layouts  5.25 us (3%)
  starting transfers between devices  3.72 us (2%)
  other arithmetic  2.79 us (1%)
    pallas_call x1, Pallas kernels, experts(): pl.pallas_call(functools.partial(expert_kernel, cap, slots), out_shape=ja...  146 us
    all_to_all x1, blocking collectives, on_device(): lax.all_to_all(mixed.astype(BF), 'pool', split_axis=0, concat_axis=0, axi...  17.7 us
    all_gather x1, blocking collectives, on_device(): routing = lax.all_gather(routing, 'pool', axis_index_groups=planes)  17.1 us
    dot_general x8, matrix products, on_device(): jnp.einsum('jtc,jcd->jtd', part, back, preferred_element_type=F32)  3.99 us
  transfers between devices with their start and end apart: 1, of which 0 were waited for; matrix products, arithmetic and copies ran while one was open for 1% of the time, Pallas kernels for 0%

profile of v3, /device:TPU:8, one launch (start us, length us, event | category | flops | bytes accessed | tf_op | source)
XLA Modules:
  0.0 198.2 jit_solution(4055478427379092751)
XLA Ops:
  0.0 0.0 copy-start
  0.0 0.0 copy-start.1
  0.0 2.3 %copy.13 = bf16[8,8,8,896]{3,2,0,1:T(8,128)(2,1)} copy(bf16[8,8,8,896]{3,2,1,0:T(8,128)(2,1)} %bitcast.45) | data formatting | bytes 1835008 | tf_op jit(solution)/shard_map/reshape | solution.py:216
  2.3 3.7 %all-to-all-start = ((bf16[8,64,896]{2,1,0:T(8,128)(2,1)}), bf16[8,64,896]{2,1,0:T(8,128)(2,1)S(1)}, u32[]{:S(2)}, u32[]{:S(2)}) async-start(bf16[8,64,896]{2,1,0:T(8,128)(2,1)} %bitcast.31), calls=%async_computation | async-start | bytes 1835008 | tf_op jit(solution)/shard_map/all_to_all | solution.py:217
  6.0 0.0 copy-done
  6.0 0.0 copy-done.1
  6.0 17.1 %all-gather.1 = s32[8,64,4]{1,2,0:T(4,128)S(1)} all-gather(s32[1,64,4]{1,2,0:T(4,128)S(1)} %add_bitcast_fusion), channel_id=2, replica_groups={{0,1,2,3,4,5,6,7},{8,9,10,11,12,13,14,15},{16,17,18,19,20,21,22,23},{24..., dimensions={0}, use_global_device_ids=true | all-gather | bytes 9216 | tf_op jit(solution)/shard_map/all_gather | solution.py:214
  23.1 0.1 fusion.87
  23.1 0.2 reduce_window_sum.22
  23.4 0.2 reduce_window_sum.23
  23.6 0.2 reduce_window_sum.27
  23.8 0.2 reduce_window_sum.32
  24.0 0.1 select_reduce_fusion.3
  24.2 0.0 all-to-all-done
  24.2 0.3 convolution_convert_fusion
  24.5 0.3 convolution_convert_fusion.1
  24.8 0.3 convolution_convert_fusion.2
  25.2 0.3 convolution_convert_fusion.3
  25.5 1.7 pad_maximum_fusion.rows_ref
  27.2 146.3 %experts.1 = bf16[4,384,896]{2,1,0:T(8,128)(2,1)} custom-call(bf16[4,384,896]{2,1,0:T(8,128)(2,1)} %pad_maximum_fusion.rows_ref, bf16[896,2048]{1,0:T(8,128)(2,1)} %gate_up_ref.1, bf16[1024,896]{1,0:T(8,128)(2,1)} %down_ref.1), custom_call_target="tpu_custom_call" | custom-call | flops 8455716864 | bytes 41943040 | tf_op jit(solution)/shard_map/experts/pallas_call | solution.py:176
  173.5 1.9 fusion.91
  175.5 0.5 fusion.9
  175.9 0.5 fusion.8
  176.4 0.5 fusion.13
  176.8 0.5 fusion.12
  177.3 0.5 fusion.11
  177.8 0.5 fusion.10
  178.2 0.5 fusion.14
  178.7 0.8 add_convert_fusion
  179.5 17.7 %all_to_all.10 = bf16[8,64,896]{2,1,0:T(8,128)(2,1)S(1)} all-to-all(bf16[8,64,896]{2,1,0:T(8,128)(2,1)S(1)} %add_convert_fusion), channel_id=1, replica_groups={{0,1,2,3,4,5,6,7},{8,9,10,11,12,13,14,15},{16,17,18,19,20,21,22,23},{24..., dimensions={0} | all-to-all | bytes 1835008 | tf_op jit(solution)/shard_map/all_to_all | solution.py:242
  197.2 1.0 copy.11
  (11 shorter events, 0.1 us)
Async XLA Ops:
  0.0 6.0 %copy-start = (s32[64,2]{0,1:T(2,128)S(1)}, s32[64,2]{0,1:T(2,128)}, u32[]{:S(2)}) copy-start(s32[64,2]{0,1:T(2,128)} %param.7) | copy-start | bytes 1540
  0.0 6.0 %copy-start.1 = (s32[64,2]{0,1:T(2,128)S(1)}, s32[64,2]{0,1:T(2,128)}, u32[]{:S(2)}) copy-start(s32[64,2]{0,1:T(2,128)} %param.6) | copy-start | bytes 1540
  2.3 21.9 %all-to-all-start = ((bf16[8,64,896]{2,1,0:T(8,128)(2,1)}), bf16[8,64,896]{2,1,0:T(8,128)(2,1)S(1)}, u32[]{:S(2)}, u32[]{:S(2)}) async-start(bf16[8,64,896]{2,1,0:T(8,128)(2,1)} %bitcast.31), calls=%async_computation | async-start | bytes 1835008 | tf_op jit(solution)/shard_map/all_to_all | solution.py:217

commit v4 on v3

--- a/solution.py
+++ b/solution.py
@@ -153,13 +153,13 @@
             outbound.append(send(result, out_ref.at[step], across_slots(step)))
 
     order = list(reversed(range(1, slots)))
-    if slots > 1:
-        dispatch(order[0])
+    for step in order[1:]:
+        dispatch(step)
     for _ in block(0):
         pass
-    for step in order[1:]:
-        dispatch(step)
-    for group in [order[:1]] + [order[first : first + 2] for first in range(1, len(order), 2)]:
+    dispatch(order[0])
+    order = order[1:] + order[:1]
+    for group in [order[first : first + 2] for first in range(0, len(order), 2)]:
         running = [block(step) for step in group]
         while running:
             running = [work for work in running if next(work, done) is not done]

time: 199 us -> 180 us (0.905)
  Pallas kernels: 146 us -> 129 us
    pallas_call x1, Pallas kernels: 146 us -> 129 us  [experts(): pl.pallas_call(functools.partial(expert_kernel, cap, slots), out_shape=ja...]
where the time goes in v4:
time: 180 us; the launch traced here: 179 us
  Pallas kernels  129 us (72%)
  blocking collectives  33.5 us (19%)
  matrix products  5.29 us (3%)
  local copies, waits for them, and re-layouts  5.25 us (3%)
  starting transfers between devices  3.72 us (2%)
  other arithmetic  2.79 us (2%)
    pallas_call x1, Pallas kernels, experts(): pl.pallas_call(functools.partial(expert_kernel, cap, slots), out_shape=ja...  129 us
    all_gather x1, blocking collectives, on_device(): routing = lax.all_gather(routing, 'pool', axis_index_groups=planes)  17.1 us
    all_to_all x1, blocking collectives, on_device(): lax.all_to_all(mixed.astype(BF), 'pool', split_axis=0, concat_axis=0, axi...  16.5 us
    dot_general x8, matrix products, on_device(): jnp.einsum('jtc,jcd->jtd', part, back, preferred_element_type=F32)  3.98 us
    all_to_all x1, starting transfers between devices, on_device(): lax.all_to_all(pieces, 'pool', split_axis=0, concat_axis=0, axis_index_gr...  3.72 us
  transfers between devices with their start and end apart: 1, of which 0 were waited for; matrix products, arithmetic and copies ran while one was open for 1% of the time, Pallas kernels for 0%

profile of v4, /device:TPU:8, one launch (start us, length us, event | category | flops | bytes accessed | tf_op | source)
XLA Modules:
  0.0 179.4 jit_solution(3194450045821575956)
XLA Ops:
  0.0 0.0 copy-start
  0.0 0.0 copy-start.1
  0.0 2.3 %copy.13 = bf16[8,8,8,896]{3,2,0,1:T(8,128)(2,1)} copy(bf16[8,8,8,896]{3,2,1,0:T(8,128)(2,1)} %bitcast.45) | data formatting | bytes 1835008 | tf_op jit(solution)/shard_map/reshape | solution.py:216
  2.3 3.7 %all-to-all-start = ((bf16[8,64,896]{2,1,0:T(8,128)(2,1)}), bf16[8,64,896]{2,1,0:T(8,128)(2,1)S(1)}, u32[]{:S(2)}, u32[]{:S(2)}) async-start(bf16[8,64,896]{2,1,0:T(8,128)(2,1)} %bitcast.31), calls=%async_computation | async-start | bytes 1835008 | tf_op jit(solution)/shard_map/all_to_all | solution.py:217
  6.0 0.0 copy-done
  6.0 0.0 copy-done.1
  6.0 17.1 %all-gather.1 = s32[8,64,4]{1,2,0:T(4,128)S(1)} all-gather(s32[1,64,4]{1,2,0:T(4,128)S(1)} %add_bitcast_fusion), channel_id=2, replica_groups={{0,1,2,3,4,5,6,7},{8,9,10,11,12,13,14,15},{16,17,18,19,20,21,22,23},{24..., dimensions={0}, use_global_device_ids=true | all-gather | bytes 9216 | tf_op jit(solution)/shard_map/all_gather | solution.py:214
  23.1 0.1 fusion.87
  23.1 0.2 reduce_window_sum.22
  23.4 0.2 reduce_window_sum.23
  23.6 0.2 reduce_window_sum.27
  23.8 0.2 reduce_window_sum.32
  24.0 0.1 select_reduce_fusion.3
  24.2 0.0 all-to-all-done
  24.2 0.3 convolution_convert_fusion
  24.5 0.3 convolution_convert_fusion.1
  24.8 0.3 convolution_convert_fusion.2
  25.2 0.3 convolution_convert_fusion.3
  25.5 1.7 pad_maximum_fusion.rows_ref
  27.2 128.6 %experts.1 = bf16[4,384,896]{2,1,0:T(8,128)(2,1)} custom-call(bf16[4,384,896]{2,1,0:T(8,128)(2,1)} %pad_maximum_fusion.rows_ref, bf16[896,2048]{1,0:T(8,128)(2,1)} %gate_up_ref.1, bf16[1024,896]{1,0:T(8,128)(2,1)} %down_ref.1), custom_call_target="tpu_custom_call" | custom-call | flops 8455716864 | bytes 41943040 | tf_op jit(solution)/shard_map/experts/pallas_call | solution.py:176
  155.8 1.9 %fusion.91 = (bf16[1,384,896]{2,1,0:T(8,128)(2,1)S(1)}, bf16[1,384,896]{2,1,0:T(8,128)(2,1)S(1)}, bf16[1,384,896]{2,1,0:T(8,128)(2,1)S(1)}, bf16[1,384,896]{2,1,0:T(8,128)(2,1)S(1)}) fusion(bf16[4,384,896]{2,1,0:T(8,128)(2,1)} %experts.1), kind=kLoop, calls=%fused_computation.143 | loop fusion | bytes 5505024 | tf_op jit(solution)/shard_map/slice | solution.py:239
  157.8 0.5 fusion.9
  158.2 0.5 fusion.8
  158.7 0.5 fusion.13
  159.2 0.5 fusion.12
  159.6 0.5 fusion.11
  160.1 0.5 fusion.10
  160.5 0.5 fusion.14
  161.0 0.8 add_convert_fusion
  161.8 16.5 %all_to_all.10 = bf16[8,64,896]{2,1,0:T(8,128)(2,1)S(1)} all-to-all(bf16[8,64,896]{2,1,0:T(8,128)(2,1)S(1)} %add_convert_fusion), channel_id=1, replica_groups={{0,1,2,3,4,5,6,7},{8,9,10,11,12,13,14,15},{16,17,18,19,20,21,22,23},{24..., dimensions={0} | all-to-all | bytes 1835008 | tf_op jit(solution)/shard_map/all_to_all | solution.py:242
  178.3 1.0 copy.11
  (11 shorter events, 0.1 us)
Async XLA Ops:
  0.0 6.0 %copy-start = (s32[64,2]{0,1:T(2,128)S(1)}, s32[64,2]{0,1:T(2,128)}, u32[]{:S(2)}) copy-start(s32[64,2]{0,1:T(2,128)} %param.7) | copy-start | bytes 1540
  0.0 6.0 %copy-start.1 = (s32[64,2]{0,1:T(2,128)S(1)}, s32[64,2]{0,1:T(2,128)}, u32[]{:S(2)}) copy-start(s32[64,2]{0,1:T(2,128)} %param.6) | copy-start | bytes 1540
  2.3 21.9 %all-to-all-start = ((bf16[8,64,896]{2,1,0:T(8,128)(2,1)}), bf16[8,64,896]{2,1,0:T(8,128)(2,1)S(1)}, u32[]{:S(2)}, u32[]{:S(2)}) async-start(bf16[8,64,896]{2,1,0:T(8,128)(2,1)} %bitcast.31), calls=%async_computation | async-start | bytes 1835008 | tf_op jit(solution)/shard_map/all_to_all | solution.py:217

commit v5 on v4

--- a/solution.py
+++ b/solution.py
@@ -18,7 +18,9 @@
 done = object()
 
 
-def expert_kernel(cap, slots, rows_ref, gate_up_ref, down_ref, out_ref, came, results, core_outs, core_ins, accs, wide_outs, wide_ins, thin_outs, thin_ins, hids, send_sems, recv_sems):
+def expert_kernel(cap, slots, *refs):
+    rows_refs = refs[:slots]
+    (gate_up_ref, down_ref, out_ref, came, results, core_outs, core_ins, accs, wide_outs, wide_ins, thin_outs, thin_ins, hids, send_sems, recv_sems) = refs[slots:]
     me = lax.axis_index("pool")
     core, x, y = me % 2, me // 2 % 2, me // 4 % 2
     by_core, by_x, by_y = me + 1 - 2 * core, me + 2 - 4 * x, me + 4 - 8 * y
@@ -62,14 +64,14 @@
     inbound, outbound = {}, []
 
     def dispatch(step):
-        inbound[step] = send_for(step, rows_ref.at[step], came.at[step - 1], across_slots(step))
+        inbound[step] = send_for(step, rows_refs[step], came.at[step - 1], across_slots(step))
 
     def block(step):
         send = functools.partial(send_for, step)
         core_out, core_in, acc, wide_out, wide_in, thin_out, thin_in, hid = (
             ref.at[step] for ref in (core_outs, core_ins, accs, wide_outs, wide_ins, thin_outs, thin_ins, hids)
         )
-        rows, result = rows_ref.at[0], out_ref.at[0]
+        rows, result = rows_refs[0], out_ref.at[0]
         if step:
             rows, result = came.at[step - 1], results.at[step - 1]
             inbound[step].wait_recv()
@@ -169,18 +171,19 @@
         copy.wait_send()
 
 
-def experts(rows, gate_up, down):
-    slots, cap, units = rows.shape[0], rows.shape[1] // SPAN, down.shape[0]
+def experts(blocks, gate_up, down):
+    slots, cap, units = len(blocks), blocks[0].shape[0] // SPAN, down.shape[0]
+    shape = (slots,) + blocks[0].shape
     copies = 15
-    flops = 2 * rows.shape[0] * rows.shape[1] * rows.shape[2] * 3 * units
+    flops = 2 * shape[0] * shape[1] * shape[2] * 3 * units
     return pl.pallas_call(
         functools.partial(expert_kernel, cap, slots),
-        out_shape=jax.ShapeDtypeStruct(rows.shape, BF),
-        in_specs=[pl.BlockSpec(memory_space=pltpu.VMEM)] * 3,
+        out_shape=jax.ShapeDtypeStruct(shape, BF),
+        in_specs=[pl.BlockSpec(memory_space=pltpu.VMEM)] * (slots + 2),
         out_specs=pl.BlockSpec(memory_space=pltpu.VMEM),
         scratch_shapes=[
-            pltpu.VMEM((max(1, slots - 1),) + rows.shape[1:], BF),
-            pltpu.VMEM((max(1, slots - 1),) + rows.shape[1:], BF),
+            pltpu.VMEM((max(1, slots - 1),) + shape[1:], BF),
+            pltpu.VMEM((max(1, slots - 1),) + shape[1:], BF),
             pltpu.VMEM((slots, 4 * cap, 2 * units), BF),
             pltpu.VMEM((slots, 4 * cap, 2 * units), BF),
             pltpu.VMEM((slots, 4 * cap, 2 * units), F32),
@@ -195,7 +198,7 @@
         compiler_params=pltpu.CompilerParams(collective_id=0, has_side_effects=True, vmem_limit_bytes=60 * 2**20),
         cost_estimate=pl.CostEstimate(flops=flops, bytes_accessed=40 * 2**20, transcendentals=0),
         name="experts",
-    )(rows, gate_up, down)
+    )(*blocks, gate_up, down)
 
 
 def on_device(tokens, slot_ids, gate_codes, gate_up, down_proj):
@@ -233,7 +236,7 @@
         block = jnp.einsum("jtc,jtd->jcd", hot.astype(BF), plane_tokens, preferred_element_type=F32)
         blocks.append(block.astype(BF).reshape(SPAN * capacity, piece))
 
-    returned = experts(jnp.stack(blocks), gate_up, down_proj)
+    returned = experts(blocks, gate_up, down_proj)
     mixed = jnp.zeros((SPAN, tok_rows, piece), F32)
     for step in range(slots):
         back = returned[step].reshape(SPAN, capacity, piece)

time: 180 us -> 181 us (level)
  matrix products: 5.29 us -> 8.73 us
    dot_general x4, matrix products: 1.31 us -> 4.74 us  [on_device(): jnp.einsum('jtc,jtd->jcd', hot.astype(BF), plane_tokens, preferred_elemen...]
where the time goes in v5:
time: 181 us
  Pallas kernels  129 us (71%)
  blocking collectives  33.6 us (19%)
  matrix products  8.73 us (5%)
  local copies, waits for them, and re-layouts  5.25 us (3%)
  starting transfers between devices  3.72 us (2%)
    pallas_call x1, Pallas kernels, experts(): pl.pallas_call(functools.partial(expert_kernel, cap, slots), out_shape=ja...  129 us
    all_gather x1, blocking collectives, on_device(): routing = lax.all_gather(routing, 'pool', axis_index_groups=planes)  17.1 us
    all_to_all x1, blocking collectives, on_device(): lax.all_to_all(mixed.astype(BF), 'pool', split_axis=0, concat_axis=0, axi...  16.5 us
    dot_general x4, matrix products, on_device(): jnp.einsum('jtc,jtd->jcd', hot.astype(BF), plane_tokens, preferred_elemen...  4.74 us
    dot_general x8, matrix products, on_device(): jnp.einsum('jtc,jcd->jtd', part, back, preferred_element_type=F32)  3.98 us
    all_to_all x1, starting transfers between devices, on_device(): lax.all_to_all(pieces, 'pool', split_axis=0, concat_axis=0, axis_index_gr...  3.72 us
  transfers between devices with their start and end apart: 1, of which 0 were waited for; matrix products, arithmetic and copies ran while one was open for 1% of the time, Pallas kernels for 0%

profile of v5, /device:TPU:8, one launch (start us, length us, event | category | flops | bytes accessed | tf_op | source)
XLA Modules:
  0.0 181.0 jit_solution(11475133442254026396)
XLA Ops:
  0.0 0.0 copy-start
  0.0 0.0 copy-start.1
  0.0 2.3 %copy.13 = bf16[8,8,8,896]{3,2,0,1:T(8,128)(2,1)} copy(bf16[8,8,8,896]{3,2,1,0:T(8,128)(2,1)} %bitcast.41) | data formatting | bytes 1835008 | tf_op jit(solution)/shard_map/reshape | solution.py:219
  2.3 3.7 %all-to-all-start = ((bf16[8,64,896]{2,1,0:T(8,128)(2,1)}), bf16[8,64,896]{2,1,0:T(8,128)(2,1)S(1)}, u32[]{:S(2)}, u32[]{:S(2)}) async-start(bf16[8,64,896]{2,1,0:T(8,128)(2,1)} %bitcast.31), calls=%async_computation | async-start | bytes 1835008 | tf_op jit(solution)/shard_map/all_to_all | solution.py:220
  6.0 0.0 copy-done
  6.0 0.0 copy-done.1
  6.0 17.1 %all-gather.1 = s32[8,64,4]{1,2,0:T(4,128)S(1)} all-gather(s32[1,64,4]{1,2,0:T(4,128)S(1)} %add_bitcast_fusion), channel_id=2, replica_groups={{0,1,2,3,4,5,6,7},{8,9,10,11,12,13,14,15},{16,17,18,19,20,21,22,23},{24..., dimensions={0}, use_global_device_ids=true | all-gather | bytes 9216 | tf_op jit(solution)/shard_map/all_gather | solution.py:217
  23.1 0.1 fusion.90
  23.1 0.2 reduce_window_sum.32
  23.4 0.2 reduce_window_sum.23
  23.6 0.2 reduce_window_sum.27
  23.8 0.2 reduce_window_sum.22
  24.0 0.1 select_reduce_fusion.3
  24.2 0.0 all-to-all-done
  24.2 1.2 convolution_convert_fusion
  25.4 1.2 convolution_convert_fusion.1
  26.5 1.2 convolution_convert_fusion.2
  27.7 1.2 convolution_convert_fusion.3
  28.9 128.6 %experts.1 = bf16[4,384,896]{2,1,0:T(8,128)(2,1)} custom-call(bf16[384,896]{1,0:T(8,128)(2,1)} %bitcast.45, bf16[384,896]{1,0:T(8,128)(2,1)} %bitcast.44, bf16[384,896]{1,0:T(8,128)(2,1)} %bitcast.43, bf16[384,896]{1,0:T(8,128)(2,1)} %bitcast.42, bf16[896,2048]{1,0:T(8,128)(2,1)} %refs_4_.1, bf16[1024,896]{1,0:T(8,128)(2,1)} %refs_5_.1), custom_call_target="tpu_custom_call" | custom-call | flops 8455716864 | bytes 41943040 | tf_op jit(solution)/shard_map/experts/pallas_call | solution.py:179
  157.5 1.9 %fusion.91 = (bf16[1,384,896]{2,1,0:T(8,128)(2,1)S(1)}, bf16[1,384,896]{2,1,0:T(8,128)(2,1)S(1)}, bf16[1,384,896]{2,1,0:T(8,128)(2,1)S(1)}, bf16[1,384,896]{2,1,0:T(8,128)(2,1)S(1)}) fusion(bf16[4,384,896]{2,1,0:T(8,128)(2,1)} %experts.1), kind=kLoop, calls=%fused_computation.142 | loop fusion | bytes 5505024 | tf_op jit(solution)/shard_map/slice | solution.py:242
  159.4 0.5 fusion.9
  159.9 0.5 fusion.8
  160.4 0.5 fusion.13
  160.8 0.5 fusion.12
  161.3 0.5 fusion.11
  161.7 0.5 fusion.10
  162.2 0.5 fusion.14
  162.7 0.8 add_convert_fusion
  163.5 16.5 %all_to_all.10 = bf16[8,64,896]{2,1,0:T(8,128)(2,1)S(1)} all-to-all(bf16[8,64,896]{2,1,0:T(8,128)(2,1)S(1)} %add_convert_fusion), channel_id=1, replica_groups={{0,1,2,3,4,5,6,7},{8,9,10,11,12,13,14,15},{16,17,18,19,20,21,22,23},{24..., dimensions={0} | all-to-all | bytes 1835008 | tf_op jit(solution)/shard_map/all_to_all | solution.py:245
  180.0 1.0 copy.11
  (11 shorter events, 0.1 us)
Async XLA Ops:
  0.0 6.0 %copy-start = (s32[64,2]{0,1:T(2,128)S(1)}, s32[64,2]{0,1:T(2,128)}, u32[]{:S(2)}) copy-start(s32[64,2]{0,1:T(2,128)} %param.7) | copy-start | bytes 1540
  0.0 6.0 %copy-start.1 = (s32[64,2]{0,1:T(2,128)S(1)}, s32[64,2]{0,1:T(2,128)}, u32[]{:S(2)}) copy-start(s32[64,2]{0,1:T(2,128)} %param.6) | copy-start | bytes 1540
  2.3 21.9 %all-to-all-start = ((bf16[8,64,896]{2,1,0:T(8,128)(2,1)}), bf16[8,64,896]{2,1,0:T(8,128)(2,1)S(1)}, u32[]{:S(2)}, u32[]{:S(2)}) async-start(bf16[8,64,896]{2,1,0:T(8,128)(2,1)} %bitcast.31), calls=%async_computation | async-start | bytes 1835008 | tf_op jit(solution)/shard_map/all_to_all | solution.py:220
